TPU v7x, 32 devices: a whole 2x2x4 slice. The times are simulated.
32 devices in a mesh: gx: 8 (over z, core), gy: 4 (over y, x).
Axes of the slice: x: 2, y: 2, z: 4, core: 2. Of those that a mesh axis runs over, the one named last changes fastest.
Arguments:
- leaf_map: float32 [8, 4, 512, 512], P('gx', 'gy'), may hold values from -0.97 to 0.97, as said below
- source_trace: float32 [8, 4, 512], P('gx', 'gy'), may hold values from -6 to 6
- tile_class: int32 [8, 4, 16], P('gx', 'gy'), may hold values from 0 to 7
- absorb_table: float32 [8], replicated, may hold values from 0.2 to 2
Outputs:
- top_map: float32 [8, 4, 192, 1536], P('gx', 'gy')
- top_out: float32 [8, 4, 192], P('gx', 'gy')
Inputs may be any that keep to these rules, and one draw needn't show every extreme that they name: `leaf_map`: each leaf map is a dense matrix whose largest singular value is at most 0.97.
All inputs are finite; a program needn't handle non-finite values.
Results may differ from a plain program's by a relative error of at most 0.000086.
Values sent between devices are 32-bit elements; how exact they have to be, the bound alone decides.
A program may use at most 128 MiB of HBM per device.

v0:
```python
import functools
import math

import jax
import jax.numpy as jnp
from jax import lax
from jax.experimental import pallas as pl
from jax.experimental.pallas import tpu as pltpu
from jax.sharding import PartitionSpec as P

DOUBLINGS = 9


def split(value):
    high = value.astype(jnp.bfloat16)
    low = (value - high.astype(jnp.float32)).astype(jnp.bfloat16)
    return high, low


def dot_parts(left, right):
    dot = functools.partial(jnp.dot, preferred_element_type=jnp.float32)
    return dot(left[0], right[0]) + (dot(left[0], right[1]) + dot(left[1], right[0]))


def dot3(left, right):
    return dot_parts(split(left), split(right))


def resolvent(product):
    size = product.shape[0]
    rows = lax.broadcasted_iota(jnp.int32, (size, size), 0)
    cols = lax.broadcasted_iota(jnp.int32, (size, size), 1)
    total = jnp.where(rows == cols, 1.0, 0.0) + product
    parts = split(product)
    power = dot_parts(parts, parts)
    for step in range(1, DOUBLINGS):
        parts = split(power)
        if step < DOUBLINGS - 1:
            sums = split(total)
            both = tuple(jnp.concatenate([s, p], axis=0) for s, p in zip(sums, parts))
            out = dot_parts(both, parts)
            total = total + out[:size]
            power = out[size:]
        else:
            total = total + dot_parts(split(total), parts)
    return total


def as_columns(row):
    return jnp.broadcast_to(row, (128, row.shape[1])).T


def gain(t_ii, o_ii, o_ri, t_h, o_h):
    t_parts = split(t_ii)
    inverse = resolvent(dot_parts(t_parts, split(o_ii)))
    g = dot3(o_ri, inverse)
    gt = dot_parts(split(g), t_parts)
    jump = as_columns(t_h) - dot_parts(t_parts, split(as_columns(o_h)))
    change = dot3(g, jump)
    short = -change.shape[0] % 128
    if short:
        change = jnp.concatenate([change, jnp.zeros((short, 128), jnp.float32)], axis=0)
    return g, gt, change.T[0:1, :]


def ordered(flag, mine, other):
    return jnp.concatenate(
        [jnp.where(flag, mine, other), jnp.where(flag, other, mine)], axis=0
    )


def kernel1(flags, own, other, h, other_h, re, ri, ie, ii, h_out):
    left, low = flags[0] == 1, flags[1] == 1
    s = own.shape[0] // 4
    e = 3 * s
    g, gt, change = gain(
        other[:, e:], own[e:, e:], own[:e, e:], other_h[...], h[:, e:]
    )
    mine = own[:e, :e] + dot3(gt, own[e:, :e])
    cross = -dot3(g, other[:, :e])
    h_new = h[:, :e] - change
    lefts = jnp.where(left, mine, cross)
    rights = jnp.where(left, cross, mine)

    def col(block, k):
        return block[:, k * s : (k + 1) * s]

    def rows(block):
        x, south, north = block[:s], block[s : 2 * s], block[2 * s :]
        return x, jnp.where(low, south, north), jnp.where(low, north, south)

    def put(k, side):
        x, y, i = rows(side)
        re[0:s, k * s : (k + 1) * s] = x
        re[s : 2 * s, k * s : (k + 1) * s] = y
        ie[:, k * s : (k + 1) * s] = i

    def put_i(k, side):
        x, y, i = rows(side)
        ri[0:s, k * s : (k + 1) * s] = x
        ri[s : 2 * s, k * s : (k + 1) * s] = y
        ii[0:s, k * s : (k + 1) * s] = i

    put(0, col(lefts, 0))
    put(1, col(rights, 0))
    for k, side in enumerate((lefts, rights)):
        put(2 + k, jnp.where(low, col(side, 1), col(side, 2)))
        put_i(k, jnp.where(low, col(side, 2), col(side, 1)))
    hx, hs, hn = col(h_new, 0), col(h_new, 1), col(h_new, 2)
    h_out[:, 0:s] = hx
    h_out[:, s : 2 * s] = jnp.where(low, hs, hn)
    hi = jnp.where(low, hn, hs)
    ii[s:, :] = jnp.broadcast_to(jnp.concatenate([hi, hi], axis=1), (8, 2 * s))


def gain2(flags, mine, mine_o, t, t_o, ri, h, g, gt, h_out):
    left = flags[0] == 1
    s = mine.shape[0] - 8

    def both(a, b):
        rows = ordered(left, a[0:s, :], b[0:s, :])
        ha, hb = a[s : s + 1, 0:s], b[s : s + 1, 0:s]
        vec = jnp.concatenate(
            [jnp.where(left, ha, hb), jnp.where(left, hb, ha)], axis=1
        )
        return rows, vec

    o_ii, o_h = both(mine, mine_o)
    t_ii, t_h = both(t, t_o)
    g[...], gt[...], change = gain(t_ii, o_ii, ri[...], t_h, o_h)
    h_out[...] = h[...] - change


def apply2(flags, re, g, gt, mine, mine_o, t, t_o, ext, inner):
    left, low, first = flags[0] == 1, flags[1] == 1, flags[2] == 1
    s = mine.shape[0]
    own = re[...] + dot3(gt[...], ordered(left, mine[...], mine_o[...]))
    cross = -dot3(g[...], ordered(left, t[...], t_o[...]))
    lows = jnp.where(low, own, cross)
    ups = jnp.where(low, cross, own)
    west = jnp.concatenate([lows[:, :s], ups[:, :s]], axis=1)
    east = jnp.concatenate([lows[:, s : 2 * s], ups[:, s : 2 * s]], axis=1)
    ext[:, : 2 * s] = jnp.where(first, west, east)
    ext[:, 2 * s : 4 * s] = lows[:, 2 * s :]
    ext[:, 4 * s :] = ups[:, 2 * s :]
    inner[...] = jnp.where(first, east, west)


def quads(flags, mine, other, n):
    left, low = flags[0] == 1, flags[1] == 1
    a = ordered(left, mine[0], other[0])
    b = ordered(left, mine[1], other[1])
    return ordered(low, a, b)


def gain3(flags, mine, other, far, far_o, ri, g, gt, change):
    low = flags[1] == 1
    n = mine.shape[1] - 8

    def both(a, b):
        rows = quads(flags, (a[0, 0:n, :], a[1, 0:n, :]), (b[0, 0:n, :], b[1, 0:n, :]), n)
        h0, h1 = a[0, n : n + 1, 0 : 2 * n], a[1, n : n + 1, 0 : 2 * n]
        vec = jnp.concatenate(
            [jnp.where(low, h0, h1), jnp.where(low, h1, h0)], axis=1
        )
        return rows, vec

    o_ii, o_h = both(mine, other)
    t_ii, t_h = both(far, far_o)
    g[...], gt[...], change[...] = gain(t_ii, o_ii, ri[...], t_h, o_h)


def apply3(scale, flags, re, g, gt, mine, other, far, far_o, out):
    first = flags[2] == 1
    n = mine.shape[1]
    e = re.shape[1]
    o_ie = quads(flags, (mine[0], mine[1]), (other[0], other[1]), n)
    t_ie = quads(flags, (far[0], far[1]), (far_o[0], far_o[1]), n)
    own = (re[...] + dot3(gt[...], o_ie)) * scale
    cross = dot3(g[...], t_ie) * (-scale)
    out[:, :e] = jnp.where(first, own, cross)
    out[:, e:] = jnp.where(first, cross, own)


def call(body, flags, operands, shapes, flops):
    outs = [jax.ShapeDtypeStruct(shape, jnp.float32) for shape in shapes]
    moved = 4 * sum(math.prod(a.shape) for a in list(operands) + outs)
    return pl.pallas_call(
        body,
        out_shape=outs,
        in_specs=[pl.BlockSpec(memory_space=pltpu.SMEM)]
        + [pl.BlockSpec(memory_space=pltpu.VMEM)] * len(operands),
        out_specs=[pl.BlockSpec(memory_space=pltpu.VMEM)] * len(outs),
        compiler_params=pltpu.CompilerParams(vmem_limit_bytes=40 * 2**20),
        cost_estimate=pl.CostEstimate(flops=flops, bytes_accessed=moved, transcendentals=0),
    )(flags, *operands)


def from_behind(block, axis, distance):
    devices = range(lax.axis_size(axis))
    route = [(i - distance, i) for i in devices if i - distance in devices]
    return lax.ppermute(block, axis, route)


def partner(value, axis, distance):
    mask = 2**distance
    pairs = [(source, source ^ mask) for source in range(lax.axis_size(axis))]
    return lax.ppermute(value, axis, pairs)


def send(value, moves):
    wide, high = lax.axis_size("gx"), lax.axis_size("gy")
    pairs = []
    for i in range(wide):
        for j in range(high):
            to = moves(i, j)
            if to is not None:
                pairs.append((i * high + j, to[0] * high + to[1]))
    return lax.ppermute(value, ("gx", "gy"), pairs)


def local(leaf_map, source_trace, tile_class, absorb_table):
    leaf_op = leaf_map[0, 0]
    s = leaf_op.shape[0] // 4
    classes = tile_class[0, 0]
    chosen = (
        classes[:, None] == jnp.arange(absorb_table.shape[0], dtype=jnp.int32)[None, :]
    ).astype(jnp.float32)
    levels = jnp.sum(chosen * absorb_table[None, :], axis=1)
    seg_width = leaf_op.shape[0] // classes.shape[0]
    spread = jnp.broadcast_to(levels[:, None], (classes.shape[0], seg_width)).reshape(-1)
    leaf_h = spread * source_trace[0, 0]
    column = lax.axis_index("gx")
    row_index = lax.axis_index("gy")
    left = column % 2 == 0
    low = row_index % 2 == 0
    first = column // 2 % 2 == 0
    flags = jnp.stack([left, low, first]).astype(jnp.int32)

    def sides(a, axis):
        w, e, so, no = jnp.split(a, 4, axis=axis)
        x, i = jnp.where(left, w, e), jnp.where(left, e, w)
        return jnp.concatenate([x, so, no, i], axis=axis)

    own = sides(sides(leaf_op, 0), 1)
    h = sides(leaf_h, 0)[None]
    other, other_h = partner((own[3 * s :], h[:, 3 * s :]), "gx", 0)
    re, ri, ie, ii, h = call(
        kernel1,
        flags,
        [own, other, h, other_h],
        [(2 * s, 4 * s), (2 * s, 2 * s), (s, 4 * s), (s + 8, 2 * s), (1, 2 * s)],
        6 * s**3 * 50,
    )

    t_ii = partner(ii, "gy", 0)
    ii_o = partner(ii, "gx", 0)
    t_ii_o = partner(t_ii, "gx", 0)
    t_ie = partner(ie, "gy", 0)
    ie_o = partner(ie, "gx", 0)
    t_ie_o = partner(t_ie, "gx", 0)
    g, gt, h = call(
        gain2,
        flags,
        [ii, ii_o, t_ii, t_ii_o, ri, h],
        [(2 * s, 2 * s), (2 * s, 2 * s), (1, 2 * s)],
        6 * (2 * s) ** 3 * 20,
    )
    ext, inner = call(
        apply2,
        flags,
        [re, g, gt, ie, ie_o, t_ie, t_ie_o],
        [(2 * s, 6 * s), (2 * s, 2 * s)],
        6 * (2 * s) ** 2 * 8 * s,
    )

    half = s // 2
    x_i, x_e = inner[:s], ext[:s]
    to_first = lambda a: jnp.where(left, a[half:], a[:half])
    keep = lambda a: jnp.where(left, a[:half], a[half:])
    holder = left != first

    def give(i, j):
        return (i ^ 1, j) if (i % 2 == 0) != (i // 2 % 2 == 0) else None

    h_x = jnp.broadcast_to(jnp.concatenate([h[:, :s], h[:, :s]], axis=1), (8, 2 * s))
    got_i = send(jnp.concatenate([to_first(x_i), h_x], axis=0), give)
    got_e = send(to_first(x_e), give)
    v_i = jnp.where(holder, jnp.concatenate([keep(x_i), h_x], axis=0), got_i)
    v_e = jnp.where(holder, keep(x_e), got_e)

    mine_i = jnp.stack([v_i, partner(v_i, "gy", 0)])
    far_i = partner(mine_i, "gx", 1)
    mine_i_o = partner(mine_i, "gx", 0)
    far_i_o = partner(far_i, "gx", 0)
    mine_e = jnp.stack([v_e, partner(v_e, "gy", 0)])
    far_e = partner(mine_e, "gx", 1)
    mine_e_o = partner(mine_e, "gx", 0)
    far_e_o = partner(far_e, "gx", 0)

    def in_first(i):
        return i // 2 % 2 == 0

    def move_a(i, j):
        if i % 2 == 0 and j % 2 == 0:
            return (i, j + 1)
        if i % 2 == 1 and j % 2 == 0 and not in_first(i):
            return (i - 1, j)
        return None

    def move_b(i, j):
        if j % 2 == 1 and i % 2 == (0 if in_first(i) else 1):
            return (i - i % 2, j - 1)
        return None

    def move_c(i, j):
        return (i + 1, j - 1) if i % 2 == 0 and j % 2 == 1 else None

    def move_d(i, j):
        if j % 2 == 1 and (i % 2 == 0 or not in_first(i)):
            return (i ^ 1, j)
        return None

    def rows_of(a):
        x, y = a[:s], a[s:]
        got_a = send(jnp.where(left, y, x), move_a)
        got_b = send(x[:half], move_b)
        got_c = send(y[:half], move_c)
        got_d = send(jnp.where(left, y[half:], x[half:]), move_d)
        lower = jnp.where(
            left,
            jnp.concatenate([jnp.where(first, x, got_a), got_b], axis=0),
            jnp.concatenate([y, got_c], axis=0),
        )
        upper = jnp.where(
            left,
            jnp.concatenate([jnp.where(first, x[half:], got_d), got_a], axis=0),
            jnp.concatenate([got_d, y], axis=0),
        )
        return jnp.where(low, lower, upper)

    row_i = rows_of(inner)
    row_h = rows_of(h[0])
    row_e = rows_of(ext)
    rows_dev = 3 * s // 2
    g, gt, change = call(
        gain3,
        flags,
        [mine_i, mine_i_o, far_i, far_i_o, row_i],
        [(rows_dev, 2 * s), (rows_dev, 2 * s), (1, 2 * s)],
        6 * (2 * s) ** 3 * 20,
    )
    h3 = row_h - change[0, :rows_dev]
    scale = math.sqrt(12 * s)
    (scaled,) = call(
        functools.partial(apply3, scale),
        flags,
        [row_e, g, gt, mine_e, mine_e_o, far_e, far_e_o],
        [(rows_dev, 12 * s)],
        6 * rows_dev * 2 * s * 12 * s,
    )

    top_h = h3
    for flag, axis, distance in ((low, "gy", 0), (left, "gx", 0), (first, "gx", 1)):
        top_h = ordered(flag, top_h, partner(top_h, axis, distance))
    edge = 2 * s
    blocks = [top_h[k * edge : (k + 1) * edge] for k in range(6)]
    from_west = from_behind(blocks[3], "gx", 4)
    from_east = from_behind(blocks[0], "gx", -4)
    from_south = from_behind(jnp.concatenate([blocks[2], blocks[5]]), "gy", 2)
    from_north = from_behind(jnp.concatenate([blocks[1], blocks[4]]), "gy", -2)
    incoming = -jnp.concatenate(
        [
            from_west,
            from_south[:edge],
            from_north[:edge],
            from_east,
            from_south[edge:],
            from_north[edge:],
        ]
    )
    out_rows = jnp.sum(scaled * (incoming / scale)[None, :], axis=1) + h3
    return (scaled[None, None], out_rows[None, None])


def solution(mesh):
    return jax.shard_map(
        local,
        mesh=mesh,
        in_specs=(P("gx", "gy", None, None), P("gx", "gy", None), P("gx", "gy", None), P()),
        out_specs=(P("gx", "gy", None, None), P("gx", "gy", None)),
        check_vma=False,
    )
```

profile of v0, /device:TPU:0, one launch (start us, length us, event | category | flops | bytes accessed | tf_op | source)
XLA Modules:
  0.0 111.8 jit_solution(3791936432988928072)
XLA Ops:
  4.3 3.8 %shard_map.59 = (f32[256,512]{1,0:T(8,128)S(1)}, f32[256,256]{1,0:T(8,128)S(1)}, f32[128,512]{1,0:T(8,128)S(1)}, f32[136,256]{1,0:T(8,128)S(1)}, f32[1,256]{1,0:T(1,128)S(1)}) custom-call(s32[3]{0:T(128)S(1)} %add_convert_fusion.flags, f32[512,512]{1,0:T(8,128)S(1)} %fusion.1.own, f32[128,512]{1,0:T(8,128)S(1)} %collective-permute-done.other, ...), custom_call_target="tpu_custom_call" | custom-call | flops 629145600 | bytes 2502144 | tf_op jit(solution)/shard_map/pallas_call | solution.py:188
  8.1 2.9 %collective-permute-start.3 = (f32[136,256]{1,0:T(8,128)S(1)}, f32[136,256]{1,0:T(8,128)S(1)}, u32[]{:S(2)}, u32[]{:S(2)}) collective-permute-start(f32[136,256]{1,0:T(8,128)S(1)} %get-tuple-element.16.mine), channel_id=1, source_target_pairs={{0,1},{1,0},{2,3},{3,2},{4,5},{5,4},{6,7},{7,6},{8,9},{9,8},{10,11... | collective-permute-start | bytes 417800 | tf_op jit(solution)/shard_map/ppermute | solution.py:208
  11.0 4.4 %collective-permute-done.3.t = f32[136,256]{1,0:T(8,128)S(1)} collective-permute-done((f32[136,256]{1,0:T(8,128)S(1)}, f32[136,256]{1,0:T(8,128)S(1)}, u32[]{:S(2)}, u32[]{:S(2)}) %collective-permute-start.3) | collective-permute-done | bytes 139296 | tf_op jit(solution)/shard_map/ppermute | solution.py:208
  15.9 4.7 %collective-permute-done.6.t = f32[128,512]{1,0:T(8,128)S(1)} collective-permute-done((f32[128,512]{1,0:T(8,128)S(1)}, f32[128,512]{1,0:T(8,128)S(1)}, u32[]{:S(2)}, u32[]{:S(2)}) %collective-permute-start.6) | collective-permute-done | bytes 262176 | tf_op jit(solution)/shard_map/ppermute | solution.py:208
  20.6 6.0 %shard_map.60 = (f32[256,256]{1,0:T(8,128)S(1)}, f32[256,256]{1,0:T(8,128)S(1)}, f32[1,256]{1,0:T(1,128)S(1)}) custom-call(s32[3]{0:T(128)S(1)} %add_convert_fusion.flags, f32[136,256]{1,0:T(8,128)S(1)} %get-tuple-element.16.mine, f32[136,256]{1,0:T(8,128)S(1)} %collective-permute-done.2.mine_o, f32[136,256]{1,0:T(8,128)S(1)} %collective-permute-done.3.t, ...), custom_call_target="tpu_custom_call" | custom-call | flops 2013265920 | bytes 1345536 | tf_op jit(solution)/shard_map/pallas_call | solution.py:188
  27.4 1.3 %collective-permute-start.27 = (f32[64]{0:T(128)S(1)}, f32[64]{0:T(128)S(1)}, u32[]{:S(2)}, u32[]{:S(2)}) collective-permute-start(f32[64]{0:T(128)S(1)} %get-tuple-element.66), channel_id=1, source_target_pairs={{1,0},{3,2},{13,8},{15,10},{17,16},{19,18},{29,24},{31,26}} | collective-permute-start | bytes 776 | tf_op jit(solution)/shard_map/ppermute | solution.py:219
  28.7 5.4 %collective-permute-start.26 = (f32[128]{0:T(128)S(1)}, f32[128]{0:T(128)S(1)}, u32[]{:S(2)}, u32[]{:S(2)}) collective-permute-start(f32[128]{0:T(128)S(1)} %broadcast_select_fusion.14), channel_id=1, source_target_pairs={{0,1},{2,3},{8,9},{10,11},{12,8},{14,10},{16,17},{18,19},{24,25},{... | collective-permute-start | bytes 1544 | tf_op jit(solution)/shard_map/ppermute | solution.py:219
  40.1 5.6 %collective-permute-start.17 = (f32[128,256]{1,0:T(8,128)S(1)}, f32[128,256]{1,0:T(8,128)S(1)}, u32[]{:S(2)}, u32[]{:S(2)}) collective-permute-start(f32[128,256]{1,0:T(8,128)S(1)} %slice_select_fusion.6), channel_id=1, source_target_pairs={{0,1},{2,3},{8,9},{10,11},{12,8},{14,10},{16,17},{18,19},{24,25},{... | collective-permute-start | bytes 393224 | tf_op jit(solution)/shard_map/ppermute | solution.py:219
  47.8 3.3 %collective-permute-start.13 = (f32[72,256]{1,0:T(8,128)S(1)}, f32[72,256]{1,0:T(8,128)S(1)}, u32[]{:S(2)}, u32[]{:S(2)}) collective-permute-start(f32[72,256]{1,0:T(8,128)S(1)} %fusion.5), channel_id=1, source_target_pairs={{0,1},{1,0},{2,3},{3,2},{4,5},{5,4},{6,7},{7,6},{8,9},{9,8},{10,11... | collective-permute-start | bytes 221192 | tf_op jit(solution)/shard_map/ppermute | solution.py:208
  51.2 4.2 %collective-permute-done.13 = f32[72,256]{1,0:T(8,128)S(1)} collective-permute-done((f32[72,256]{1,0:T(8,128)S(1)}, f32[72,256]{1,0:T(8,128)S(1)}, u32[]{:S(2)}, u32[]{:S(2)}) %collective-permute-start.13) | collective-permute-done | bytes 73760 | tf_op jit(solution)/shard_map/ppermute | solution.py:208
  57.4 4.0 %collective-permute-done.15.far = f32[2,72,256]{2,1,0:T(8,128)S(1)} collective-permute-done((f32[2,72,256]{2,1,0:T(8,128)S(1)}, f32[2,72,256]{2,1,0:T(8,128)S(1)}, u32[]{:S(2)}, u32[]{:S(2)}) %collective-permute-start.15) | collective-permute-done | bytes 147488 | tf_op jit(solution)/shard_map/ppermute | solution.py:208
  61.5 3.2 %collective-permute-start.8 = (f32[128,768]{1,0:T(8,128)S(1)}, f32[128,768]{1,0:T(8,128)S(1)}, u32[]{:S(2)}, u32[]{:S(2)}) collective-permute-start(f32[128,768]{1,0:T(8,128)S(1)} %slice_select_fusion.1), channel_id=1, source_target_pairs={{0,1},{2,3},{8,9},{10,11},{12,8},{14,10},{16,17},{18,19},{24,25},{... | collective-permute-start | bytes 1179656 | tf_op jit(solution)/shard_map/ppermute | solution.py:219
  66.7 6.1 %shard_map.62 = (f32[192,256]{1,0:T(8,128)S(1)}, f32[192,256]{1,0:T(8,128)S(1)}, f32[1,256]{1,0:T(1,128)S(1)}) custom-call(s32[3]{0:T(128)S(1)} %add_convert_fusion.flags, f32[2,72,256]{2,1,0:T(8,128)S(1)} %pad_maximum_fusion.3.mine, f32[2,72,256]{2,1,0:T(8,128)S(1)} %collective-permute-done.14.other, f32[2,72,256]{2,1,0:T(8,128)S(1)} %collective-permute-done.15.far, ...), custom_call_target="tpu_custom_call" | custom-call | flops 2013265920 | bytes 1180672 | tf_op jit(solution)/shard_map/pallas_call | solution.py:188
  73.7 3.9 %collective-permute-start.30 = (f32[192]{0:T(256)S(1)}, f32[192]{0:T(256)S(1)}, u32[]{:S(2)}, u32[]{:S(2)}) collective-permute-start(f32[192]{0:T(256)S(1)} %fusion.9), channel_id=1, source_target_pairs={{0,1},{1,0},{2,3},{3,2},{4,5},{5,4},{6,7},{7,6},{8,9},{9,8},{10,11... | collective-permute-start | bytes 2312 | tf_op jit(solution)/shard_map/ppermute | solution.py:208
  77.7 1.5 %collective-permute-done.30 = f32[192]{0:T(256)S(1)} collective-permute-done((f32[192]{0:T(256)S(1)}, f32[192]{0:T(256)S(1)}, u32[]{:S(2)}, u32[]{:S(2)}) %collective-permute-start.30) | collective-permute-done | bytes 800 | tf_op jit(solution)/shard_map/ppermute | solution.py:208
  81.2 1.3 %collective-permute-start.32 = (f32[768]{0:T(1024)S(1)}, f32[768]{0:T(1024)S(1)}, u32[]{:S(2)}, u32[]{:S(2)}) collective-permute-start(f32[768]{0:T(1024)S(1)} %pad_maximum_fusion.6), channel_id=1, source_target_pairs={{0,8},{4,12},{8,0},{12,4},{16,24},{20,28},{24,16},{28,20},{1,9},{5... | collective-permute-start | bytes 9224 | tf_op jit(solution)/shard_map/ppermute | solution.py:208
  82.7 7.2 %collective-permute-done.32 = f32[768]{0:T(1024)S(1)} collective-permute-done((f32[768]{0:T(1024)S(1)}, f32[768]{0:T(1024)S(1)}, u32[]{:S(2)}, u32[]{:S(2)}) %collective-permute-start.32) | collective-permute-done | bytes 3104 | tf_op jit(solution)/shard_map/ppermute | solution.py:208
  89.9 4.5 %collective-permute-start.33 = (f32[256]{0:T(256)S(1)}, f32[256]{0:T(256)S(1)}, u32[]{:S(2)}, u32[]{:S(2)}) collective-permute-start(f32[256]{0:T(256)S(1)} %get-tuple-element.55), channel_id=1, source_target_pairs={{0,16},{4,20},{8,24},{12,28},{1,17},{5,21},{9,25},{13,29},{2,18},{... | collective-permute-start | bytes 3080 | tf_op jit(solution)/shard_map/ppermute | solution.py:202
  94.4 3.4 %collective-permute-start.34 = (f32[512]{0:T(512)S(1)}, f32[512]{0:T(512)S(1)}, u32[]{:S(2)}, u32[]{:S(2)}) collective-permute-start(f32[512]{0:T(512)S(1)} %pad_maximum_fusion.9), channel_id=1, source_target_pairs={{0,2},{1,3},{4,6},{5,7},{8,10},{9,11},{12,14},{13,15},{16,18},{17,... | collective-permute-start | bytes 6152 | tf_op jit(solution)/shard_map/ppermute | solution.py:202
  100.5 2.8 %collective-permute-done.35 = f32[512]{0:T(512)S(1)} collective-permute-done((f32[512]{0:T(512)S(1)}, f32[512]{0:T(512)S(1)}, u32[]{:S(2)}, u32[]{:S(2)}) %collective-permute-start.35) | collective-permute-done | bytes 2080 | tf_op jit(solution)/shard_map/ppermute | solution.py:202
  103.3 2.2 %collective-permute-done.36 = f32[256]{0:T(256)S(1)} collective-permute-done((f32[256]{0:T(256)S(1)}, f32[256]{0:T(256)S(1)}, u32[]{:S(2)}, u32[]{:S(2)}) %collective-permute-start.36) | collective-permute-done | bytes 1056 | tf_op jit(solution)/shard_map/ppermute | solution.py:202
  105.6 1.7 %collective-permute-done.25.far_o = f32[2,64,768]{2,1,0:T(8,128)S(1)} collective-permute-done((f32[2,64,768]{2,1,0:T(8,128)S(1)}, f32[2,64,768]{2,1,0:T(8,128)S(1)}, u32[]{:S(2)}, u32[]{:S(2)}) %collective-permute-start.25) | collective-permute-done | bytes 393248 | tf_op jit(solution)/shard_map/ppermute | solution.py:208
  107.3 2.4 %shard_map.63 = f32[192,1536]{1,0:T(8,128)} custom-call(s32[3]{0:T(128)S(1)} %add_convert_fusion.flags, f32[192,768]{1,0:T(8,128)S(1)} %fusion.3.re, f32[192,256]{1,0:T(8,128)S(1)} %get-tuple-element.25.g, f32[192,256]{1,0:T(8,128)S(1)} %get-tuple-element.26.gt, f32[2,64,768]{2,1,0:T(8,128)S(1)} %pad_maximum_fusion.mine, ...), custom_call_target="tpu_custom_call" | custom-call | flops 452984832 | bytes 3735552 | tf_op jit(solution)/shard_map/pallas_call | solution.py:188
  109.7 1.4 %multiply_reduce_fusion = f32[192]{0:T(256)S(1)} fusion(f32[192,1536]{1,0:T(8,128)} %shard_map.63, f32[1536]{0:T(1024)S(1)} %negate_multiply_fusion), kind=kLoop, calls=%fused_computation.2 | loop fusion | flops 589632 | bytes 1186560 | tf_op jit(solution)/shard_map/reduce_sum | solution.py:382
  (118 shorter events, 23.4 us)
Async XLA Ops:
  8.1 7.3 %collective-permute-start.3 = (f32[136,256]{1,0:T(8,128)S(1)}, f32[136,256]{1,0:T(8,128)S(1)}, u32[]{:S(2)}, u32[]{:S(2)}) collective-permute-start(f32[136,256]{1,0:T(8,128)S(1)} %get-tuple-element.16.mine), channel_id=1, source_target_pairs={{0,1},{1,0},{2,3},{3,2},{4,5},{5,4},{6,7},{7,6},{8,9},{9,8},{10,11... | collective-permute-start | bytes 417800 | tf_op jit(solution)/shard_map/ppermute | solution.py:208
  11.0 9.7 %collective-permute-start.6 = (f32[128,512]{1,0:T(8,128)S(1)}, f32[128,512]{1,0:T(8,128)S(1)}, u32[]{:S(2)}, u32[]{:S(2)}) collective-permute-start(f32[128,512]{1,0:T(8,128)S(1)} %get-tuple-element.21.mine), channel_id=1, source_target_pairs={{0,1},{1,0},{2,3},{3,2},{4,5},{5,4},{6,7},{7,6},{8,9},{9,8},{10,11... | collective-permute-start | bytes 786440 | tf_op jit(solution)/shard_map/ppermute | solution.py:208
  11.0 9.6 %collective-permute-start.2 = (f32[136,256]{1,0:T(8,128)S(1)}, f32[136,256]{1,0:T(8,128)S(1)}, u32[]{:S(2)}, u32[]{:S(2)}) collective-permute-start(f32[136,256]{1,0:T(8,128)S(1)} %get-tuple-element.16.mine), channel_id=1, source_target_pairs={{0,4},{4,0},{8,12},{12,8},{16,20},{20,16},{24,28},{28,24},{1,5},{5... | collective-permute-start | bytes 417800 | tf_op jit(solution)/shard_map/ppermute | solution.py:208
  15.4 20.0 %collective-permute-start.5 = (f32[128,512]{1,0:T(8,128)S(1)}, f32[128,512]{1,0:T(8,128)S(1)}, u32[]{:S(2)}, u32[]{:S(2)}) collective-permute-start(f32[128,512]{1,0:T(8,128)S(1)} %get-tuple-element.21.mine), channel_id=1, source_target_pairs={{0,4},{4,0},{8,12},{12,8},{16,20},{20,16},{24,28},{28,24},{1,5},{5... | collective-permute-start | bytes 786440 | tf_op jit(solution)/shard_map/ppermute | solution.py:208
  20.6 14.8 %collective-permute-start.7 = (f32[128,512]{1,0:T(8,128)S(1)}, f32[128,512]{1,0:T(8,128)S(1)}, u32[]{:S(2)}, u32[]{:S(2)}) collective-permute-start(f32[128,512]{1,0:T(8,128)S(1)} %collective-permute-done.6.t), channel_id=1, source_target_pairs={{0,4},{4,0},{8,12},{12,8},{16,20},{20,16},{24,28},{28,24},{1,5},{5... | collective-permute-start | bytes 786440 | tf_op jit(solution)/shard_map/ppermute | solution.py:208
  26.8 7.4 %collective-permute-start.29 = (f32[64]{0:T(128)S(1)}, f32[64]{0:T(128)S(1)}, u32[]{:S(2)}, u32[]{:S(2)}) collective-permute-start(f32[64]{0:T(128)S(1)} %broadcast_select_fusion.7), channel_id=1, source_target_pairs={{1,5},{3,7},{9,13},{11,15},{13,9},{15,11},{17,21},{19,23},{25,29},... | collective-permute-start | bytes 776 | tf_op jit(solution)/shard_map/ppermute | solution.py:219
  27.4 45.3 %collective-permute-start.27 = (f32[64]{0:T(128)S(1)}, f32[64]{0:T(128)S(1)}, u32[]{:S(2)}, u32[]{:S(2)}) collective-permute-start(f32[64]{0:T(128)S(1)} %get-tuple-element.66), channel_id=1, source_target_pairs={{1,0},{3,2},{13,8},{15,10},{17,16},{19,18},{29,24},{31,26}} | collective-permute-start | bytes 776 | tf_op jit(solution)/shard_map/ppermute | solution.py:219
  28.7 6.7 %collective-permute-start.26 = (f32[128]{0:T(128)S(1)}, f32[128]{0:T(128)S(1)}, u32[]{:S(2)}, u32[]{:S(2)}) collective-permute-start(f32[128]{0:T(128)S(1)} %broadcast_select_fusion.14), channel_id=1, source_target_pairs={{0,1},{2,3},{8,9},{10,11},{12,8},{14,10},{16,17},{18,19},{24,25},{... | collective-permute-start | bytes 1544 | tf_op jit(solution)/shard_map/ppermute | solution.py:219
  37.5 9.6 %collective-permute-start.12 = (f32[72,256]{1,0:T(8,128)S(1)}, f32[72,256]{1,0:T(8,128)S(1)}, u32[]{:S(2)}, u32[]{:S(2)}) collective-permute-start(f32[72,256]{1,0:T(8,128)S(1)} %pad_maximum_fusion.4), channel_id=1, source_target_pairs={{4,0},{5,1},{6,2},{7,3},{8,12},{9,13},{10,14},{11,15},{20,16},{21,... | collective-permute-start | bytes 221192 | tf_op jit(solution)/shard_map/ppermute | solution.py:219
  38.8 8.9 %collective-permute-start.21 = (f32[64,768]{1,0:T(8,128)S(1)}, f32[64,768]{1,0:T(8,128)S(1)}, u32[]{:S(2)}, u32[]{:S(2)}) collective-permute-start(f32[64,768]{1,0:T(8,128)S(1)} %slice_select_fusion.3), channel_id=1, source_target_pairs={{4,0},{5,1},{6,2},{7,3},{8,12},{9,13},{10,14},{11,15},{20,16},{21,... | collective-permute-start | bytes 589832 | tf_op jit(solution)/shard_map/ppermute | solution.py:219
  40.1 16.1 %collective-permute-start.17 = (f32[128,256]{1,0:T(8,128)S(1)}, f32[128,256]{1,0:T(8,128)S(1)}, u32[]{:S(2)}, u32[]{:S(2)}) collective-permute-start(f32[128,256]{1,0:T(8,128)S(1)} %slice_select_fusion.6), channel_id=1, source_target_pairs={{0,1},{2,3},{8,9},{10,11},{12,8},{14,10},{16,17},{18,19},{24,25},{... | collective-permute-start | bytes 393224 | tf_op jit(solution)/shard_map/ppermute | solution.py:219
  45.8 10.6 %collective-permute-start.18 = (f32[64,256]{1,0:T(8,128)S(1)}, f32[64,256]{1,0:T(8,128)S(1)}, u32[]{:S(2)}, u32[]{:S(2)}) collective-permute-start(f32[64,256]{1,0:T(8,128)S(1)} %get-tuple-element.45), channel_id=1, source_target_pairs={{1,0},{3,2},{13,8},{15,10},{17,16},{19,18},{29,24},{31,26}} | collective-permute-start | bytes 196616 | tf_op jit(solution)/shard_map/ppermute | solution.py:219
  47.1 10.0 %collective-permute-start.19 = (f32[64,256]{1,0:T(8,128)S(1)}, f32[64,256]{1,0:T(8,128)S(1)}, u32[]{:S(2)}, u32[]{:S(2)}) collective-permute-start(f32[64,256]{1,0:T(8,128)S(1)} %get-tuple-element.43), channel_id=1, source_target_pairs={{1,4},{3,6},{9,12},{11,14},{17,20},{19,22},{25,28},{27,30}} | collective-permute-start | bytes 196616 | tf_op jit(solution)/shard_map/ppermute | solution.py:219
  47.8 7.6 %collective-permute-start.13 = (f32[72,256]{1,0:T(8,128)S(1)}, f32[72,256]{1,0:T(8,128)S(1)}, u32[]{:S(2)}, u32[]{:S(2)}) collective-permute-start(f32[72,256]{1,0:T(8,128)S(1)} %fusion.5), channel_id=1, source_target_pairs={{0,1},{1,0},{2,3},{3,2},{4,5},{5,4},{6,7},{7,6},{8,9},{9,8},{10,11... | collective-permute-start | bytes 221192 | tf_op jit(solution)/shard_map/ppermute | solution.py:208
  56.4 17.1 %collective-permute-start.28 = (f32[64]{0:T(128)S(1)}, f32[64]{0:T(128)S(1)}, u32[]{:S(2)}, u32[]{:S(2)}) collective-permute-start(f32[64]{0:T(128)S(1)} %get-tuple-element.65), channel_id=1, source_target_pairs={{1,4},{3,6},{9,12},{11,14},{17,20},{19,22},{25,28},{27,30}} | collective-permute-start | bytes 776 | tf_op jit(solution)/shard_map/ppermute | solution.py:219
  57.0 7.7 %collective-permute-start.14 = (f32[2,72,256]{2,1,0:T(8,128)S(1)}, f32[2,72,256]{2,1,0:T(8,128)S(1)}, u32[]{:S(2)}, u32[]{:S(2)}) collective-permute-start(f32[2,72,256]{2,1,0:T(8,128)S(1)} %pad_maximum_fusion.3.mine), channel_id=1, source_target_pairs={{0,4},{4,0},{8,12},{12,8},{16,20},{20,16},{24,28},{28,24},{1,5},{5... | collective-permute-start | bytes 442376 | tf_op jit(solution)/shard_map/ppermute | solution.py:208
  61.5 12.1 %collective-permute-start.8 = (f32[128,768]{1,0:T(8,128)S(1)}, f32[128,768]{1,0:T(8,128)S(1)}, u32[]{:S(2)}, u32[]{:S(2)}) collective-permute-start(f32[128,768]{1,0:T(8,128)S(1)} %slice_select_fusion.1), channel_id=1, source_target_pairs={{0,1},{2,3},{8,9},{10,11},{12,8},{14,10},{16,17},{18,19},{24,25},{... | collective-permute-start | bytes 1179656 | tf_op jit(solution)/shard_map/ppermute | solution.py:219
  64.7 17.8 %collective-permute-start.9 = (f32[64,768]{1,0:T(8,128)S(1)}, f32[64,768]{1,0:T(8,128)S(1)}, u32[]{:S(2)}, u32[]{:S(2)}) collective-permute-start(f32[64,768]{1,0:T(8,128)S(1)} %get-tuple-element.38), channel_id=1, source_target_pairs={{1,0},{3,2},{13,8},{15,10},{17,16},{19,18},{29,24},{31,26}} | collective-permute-start | bytes 589832 | tf_op jit(solution)/shard_map/ppermute | solution.py:219
  66.0 16.5 %collective-permute-start.10 = (f32[64,768]{1,0:T(8,128)S(1)}, f32[64,768]{1,0:T(8,128)S(1)}, u32[]{:S(2)}, u32[]{:S(2)}) collective-permute-start(f32[64,768]{1,0:T(8,128)S(1)} %get-tuple-element.37), channel_id=1, source_target_pairs={{1,4},{3,6},{9,12},{11,14},{17,20},{19,22},{25,28},{27,30}} | collective-permute-start | bytes 589832 | tf_op jit(solution)/shard_map/ppermute | solution.py:219
  72.8 7.2 %collective-permute-start.11 = (f32[64,768]{1,0:T(8,128)S(1)}, f32[64,768]{1,0:T(8,128)S(1)}, u32[]{:S(2)}, u32[]{:S(2)}) collective-permute-start(f32[64,768]{1,0:T(8,128)S(1)} %get-tuple-element.36), channel_id=1, source_target_pairs={{1,5},{3,7},{9,13},{11,15},{13,9},{15,11},{17,21},{19,23},{25,29},... | collective-permute-start | bytes 589832 | tf_op jit(solution)/shard_map/ppermute | solution.py:219
  73.5 32.1 %collective-permute-start.23 = (f32[2,64,768]{2,1,0:T(8,128)S(1)}, f32[2,64,768]{2,1,0:T(8,128)S(1)}, u32[]{:S(2)}, u32[]{:S(2)}) collective-permute-start(f32[2,64,768]{2,1,0:T(8,128)S(1)} %pad_maximum_fusion.mine), channel_id=1, source_target_pairs={{0,4},{4,0},{8,12},{12,8},{16,20},{20,16},{24,28},{28,24},{1,5},{5... | collective-permute-start | bytes 1179656 | tf_op jit(solution)/shard_map/ppermute | solution.py:208
  79.1 26.4 %collective-permute-start.24 = (f32[2,64,768]{2,1,0:T(8,128)S(1)}, f32[2,64,768]{2,1,0:T(8,128)S(1)}, u32[]{:S(2)}, u32[]{:S(2)}) collective-permute-start(f32[2,64,768]{2,1,0:T(8,128)S(1)} %pad_maximum_fusion.mine), channel_id=1, source_target_pairs={{0,8},{4,12},{8,0},{12,4},{16,24},{20,28},{24,16},{28,20},{1,9},{5... | collective-permute-start | bytes 1179656 | tf_op jit(solution)/shard_map/ppermute | solution.py:208
  81.2 8.6 %collective-permute-start.32 = (f32[768]{0:T(1024)S(1)}, f32[768]{0:T(1024)S(1)}, u32[]{:S(2)}, u32[]{:S(2)}) collective-permute-start(f32[768]{0:T(1024)S(1)} %pad_maximum_fusion.6), channel_id=1, source_target_pairs={{0,8},{4,12},{8,0},{12,4},{16,24},{20,28},{24,16},{28,20},{1,9},{5... | collective-permute-start | bytes 9224 | tf_op jit(solution)/shard_map/ppermute | solution.py:208
  89.9 9.3 %collective-permute-start.33 = (f32[256]{0:T(256)S(1)}, f32[256]{0:T(256)S(1)}, u32[]{:S(2)}, u32[]{:S(2)}) collective-permute-start(f32[256]{0:T(256)S(1)} %get-tuple-element.55), channel_id=1, source_target_pairs={{0,16},{4,20},{8,24},{12,28},{1,17},{5,21},{9,25},{13,29},{2,18},{... | collective-permute-start | bytes 3080 | tf_op jit(solution)/shard_map/ppermute | solution.py:202
  (16 other events, 53.9 us)
where the time goes:
time: 112 us
  starting transfers between devices  50.4 us (45%)
  waiting for transfers between devices  35.8 us (32%)
  Pallas kernels  19.4 us (17%)
  other arithmetic  4.7 us (4%)
  between operations  1.25 us (1%)
    ppermute x19, waiting for transfers between devices, partner(): return lax.ppermute(value, axis, pairs)  29.5 us
    ppermute x14, starting transfers between devices, send(): return lax.ppermute(value, ('gx', 'gy'), pairs)  24.6 us
    pallas_call x5, Pallas kernels, call(): pl.pallas_call(body, out_shape=outs, in_specs=[pl.BlockSpec(memory_space=...  19.4 us
    ppermute x19, starting transfers between devices, partner(): return lax.ppermute(value, axis, pairs)  15.2 us
    ppermute x4, starting transfers between devices, from_behind(): return lax.ppermute(block, axis, route)  10.5 us
    ppermute x4, waiting for transfers between devices, from_behind(): return lax.ppermute(block, axis, route)  5.02 us
  transfers between devices with their start and end apart: 37, of which 12 were waited for; matrix products, arithmetic and copies ran while one was open for 1% of the time, Pallas kernels for 12%

commit v1 on v0

--- a/solution.py
+++ b/solution.py
@@ -51,11 +51,18 @@
 
 
 def gain(t_ii, o_ii, o_ri, t_h, o_h):
+    return apply_gain(*interface(t_ii, o_ii, t_h, o_h), t_ii, o_ri)
+
+
+def interface(t_ii, o_ii, t_h, o_h):
     t_parts = split(t_ii)
     inverse = resolvent(dot_parts(t_parts, split(o_ii)))
+    return inverse, as_columns(t_h) - dot_parts(t_parts, split(as_columns(o_h)))
+
+
+def apply_gain(inverse, jump, t_ii, o_ri):
     g = dot3(o_ri, inverse)
-    gt = dot_parts(split(g), t_parts)
-    jump = as_columns(t_h) - dot_parts(t_parts, split(as_columns(o_h)))
+    gt = dot3(g, t_ii)
     change = dot3(g, jump)
     short = -change.shape[0] % 128
     if short:
@@ -146,36 +153,40 @@
     inner[...] = jnp.where(first, east, west)
 
 
-def quads(flags, mine, other, n):
+def quads(flags, mine, other):
     left, low = flags[0] == 1, flags[1] == 1
     a = ordered(left, mine[0], other[0])
     b = ordered(left, mine[1], other[1])
     return ordered(low, a, b)
 
 
-def gain3(flags, mine, other, far, far_o, ri, g, gt, change):
+def solve3(flags, m0, m1, o0, o1, f0, f1, p0, p1, inverse, jump, t_out):
     low = flags[1] == 1
-    n = mine.shape[1] - 8
+    n = m0.shape[0] - 8
 
     def both(a, b):
-        rows = quads(flags, (a[0, 0:n, :], a[1, 0:n, :]), (b[0, 0:n, :], b[1, 0:n, :]), n)
-        h0, h1 = a[0, n : n + 1, 0 : 2 * n], a[1, n : n + 1, 0 : 2 * n]
+        rows = quads(flags, [r[0:n, :] for r in a], [r[0:n, :] for r in b])
+        h0, h1 = a[0][n : n + 1, 0 : 2 * n], a[1][n : n + 1, 0 : 2 * n]
         vec = jnp.concatenate(
             [jnp.where(low, h0, h1), jnp.where(low, h1, h0)], axis=1
         )
         return rows, vec
 
-    o_ii, o_h = both(mine, other)
-    t_ii, t_h = both(far, far_o)
-    g[...], gt[...], change[...] = gain(t_ii, o_ii, ri[...], t_h, o_h)
-
-
-def apply3(scale, flags, re, g, gt, mine, other, far, far_o, out):
+    o_ii, o_h = both((m0, m1), (o0, o1))
+    t_ii, t_h = both((f0, f1), (p0, p1))
+    inverse[...], jump[...] = interface(t_ii, o_ii, t_h, o_h)
+    t_out[...] = t_ii
+
+
+def gain3(flags, inverse, jump, t_ii, ri, g, gt, change):
+    g[...], gt[...], change[...] = apply_gain(inverse[...], jump[...], t_ii[...], ri[...])
+
+
+def apply3(scale, flags, re, g, gt, m0, m1, o0, o1, f0, f1, p0, p1, out):
     first = flags[2] == 1
-    n = mine.shape[1]
     e = re.shape[1]
-    o_ie = quads(flags, (mine[0], mine[1]), (other[0], other[1]), n)
-    t_ie = quads(flags, (far[0], far[1]), (far_o[0], far_o[1]), n)
+    o_ie = quads(flags, (m0[...], m1[...]), (o0[...], o1[...]))
+    t_ie = quads(flags, (f0[...], f1[...]), (p0[...], p1[...]))
     own = (re[...] + dot3(gt[...], o_ie)) * scale
     cross = dot3(g[...], t_ie) * (-scale)
     out[:, :e] = jnp.where(first, own, cross)
@@ -206,6 +217,10 @@
     mask = 2**distance
     pairs = [(source, source ^ mask) for source in range(lax.axis_size(axis))]
     return lax.ppermute(value, axis, pairs)
+
+
+def after(value, earlier):
+    return lax.optimization_barrier((value, earlier))[0]
 
 
 def send(value, moves):
@@ -256,7 +271,7 @@
     t_ii = partner(ii, "gy", 0)
     ii_o = partner(ii, "gx", 0)
     t_ii_o = partner(t_ii, "gx", 0)
-    t_ie = partner(ie, "gy", 0)
+    t_ie = partner(after(ie, t_ii), "gy", 0)
     ie_o = partner(ie, "gx", 0)
     t_ie_o = partner(t_ie, "gx", 0)
     g, gt, h = call(
@@ -285,18 +300,20 @@
 
     h_x = jnp.broadcast_to(jnp.concatenate([h[:, :s], h[:, :s]], axis=1), (8, 2 * s))
     got_i = send(jnp.concatenate([to_first(x_i), h_x], axis=0), give)
-    got_e = send(to_first(x_e), give)
+    got_e = send(after(to_first(x_e), got_i), give)
     v_i = jnp.where(holder, jnp.concatenate([keep(x_i), h_x], axis=0), got_i)
     v_e = jnp.where(holder, keep(x_e), got_e)
 
-    mine_i = jnp.stack([v_i, partner(v_i, "gy", 0)])
-    far_i = partner(mine_i, "gx", 1)
-    mine_i_o = partner(mine_i, "gx", 0)
-    far_i_o = partner(far_i, "gx", 0)
-    mine_e = jnp.stack([v_e, partner(v_e, "gy", 0)])
-    far_e = partner(mine_e, "gx", 1)
-    mine_e_o = partner(mine_e, "gx", 0)
-    far_e_o = partner(far_e, "gx", 0)
+    def spread_out(v):
+        beside = partner(v, "gy", 0)
+        far = partner(v, "gx", 1)
+        far_beside = partner(beside, "gx", 1)
+        pieces = [v, beside, far, far_beside]
+        shared = [partner(piece, "gx", 0) for piece in pieces]
+        return pieces[:2] + shared[:2] + pieces[2:] + shared[2:]
+
+    quad_i = spread_out(v_i)
+    quad_e = spread_out(after(v_e, quad_i[5]))
 
     def in_first(i):
         return i // 2 % 2 == 0
@@ -339,23 +356,31 @@
         )
         return jnp.where(low, lower, upper)
 
-    row_i = rows_of(inner)
+    row_i = rows_of(after(inner, quad_i[1]))
     row_h = rows_of(h[0])
-    row_e = rows_of(ext)
+    row_e = rows_of(after(ext, quad_i[5]))
     rows_dev = 3 * s // 2
+    solved = call(
+        solve3,
+        flags,
+        quad_i,
+        [(2 * s, 2 * s), (2 * s, 128), (2 * s, 2 * s)],
+        6 * (2 * s) ** 3 * 40,
+    )
+    row_i = after(row_i, (quad_e[1], quad_e[4], row_e))
     g, gt, change = call(
         gain3,
         flags,
-        [mine_i, mine_i_o, far_i, far_i_o, row_i],
+        [*solved, row_i],
         [(rows_dev, 2 * s), (rows_dev, 2 * s), (1, 2 * s)],
-        6 * (2 * s) ** 3 * 20,
+        6 * (2 * s) ** 3 * 2,
     )
     h3 = row_h - change[0, :rows_dev]
     scale = math.sqrt(12 * s)
     (scaled,) = call(
         functools.partial(apply3, scale),
         flags,
-        [row_e, g, gt, mine_e, mine_e_o, far_e, far_e_o],
+        [row_e, g, gt, *quad_e],
         [(rows_dev, 12 * s)],
         6 * rows_dev * 2 * s * 12 * s,
     )
@@ -369,6 +394,9 @@
     from_east = from_behind(blocks[0], "gx", -4)
     from_south = from_behind(jnp.concatenate([blocks[2], blocks[5]]), "gy", 2)
     from_north = from_behind(jnp.concatenate([blocks[1], blocks[4]]), "gy", -2)
+    from_west, from_east, from_south, from_north = lax.optimization_barrier(
+        (from_west, from_east, from_south, from_north)
+    )
     incoming = -jnp.concatenate(
         [
             from_west,

time: 112 us -> 113 us (level)
  starting transfers between devices: 50.4 us -> 53 us
  waiting for transfers between devices: 35.8 us -> 33.7 us
    ppermute x19 -> x25, waiting for transfers between devices: 29.5 us -> 18.2 us  [partner(): return lax.ppermute(value, axis, pairs)]
    ppermute x14, waiting for transfers between devices: 1.23 us -> 11.4 us  [send(): return lax.ppermute(value, ('gx', 'gy'), pairs)]
    ppermute x19 -> x25, starting transfers between devices: 15.2 us -> 19.8 us  [partner(): return lax.ppermute(value, axis, pairs)]
    ppermute x14, starting transfers between devices: 24.6 us -> 21.5 us  [send(): return lax.ppermute(value, ('gx', 'gy'), pairs)]
    pallas_call x5 -> x6, Pallas kernels: 19.4 us -> 19.9 us  [call(): pl.pallas_call(body, out_shape=outs, in_specs=[pl.BlockSpec(memory_space=...]
  transfers between devices with their start and end apart: 37 -> 43, of which waited for: 12 -> 13; matrix products, arithmetic and copies ran while one was open for 1% -> 1% of each run, Pallas kernels for 12% -> 12%
where the time goes in v1:
time: 113 us
  starting transfers between devices  53 us (47%)
  waiting for transfers between devices  33.7 us (30%)
  Pallas kernels  19.9 us (18%)
  other arithmetic  4.68 us (4%)
  between operations  1.29 us (1%)
    ppermute x14, starting transfers between devices, send(): return lax.ppermute(value, ('gx', 'gy'), pairs)  21.5 us
    pallas_call x6, Pallas kernels, call(): pl.pallas_call(body, out_shape=outs, in_specs=[pl.BlockSpec(memory_space=...  19.9 us
    ppermute x25, starting transfers between devices, partner(): return lax.ppermute(value, axis, pairs)  19.8 us
    ppermute x25, waiting for transfers between devices, partner(): return lax.ppermute(value, axis, pairs)  18.2 us
    ppermute x4, starting transfers between devices, from_behind(): return lax.ppermute(block, axis, route)  11.6 us
    ppermute x14, waiting for transfers between devices, send(): return lax.ppermute(value, ('gx', 'gy'), pairs)  11.4 us
    ppermute x4, waiting for transfers between devices, from_behind(): return lax.ppermute(block, axis, route)  4.15 us
  transfers between devices with their start and end apart: 43, of which 13 were waited for; matrix products, arithmetic and copies ran while one was open for 1% of the time, Pallas kernels for 12%

profile of v1, /device:TPU:0, one launch (start us, length us, event | category | flops | bytes accessed | tf_op | source)
XLA Modules:
  0.0 112.9 jit_solution(617714180657201651)
XLA Ops:
  4.3 3.8 %shard_map.59 = (f32[256,512]{1,0:T(8,128)S(1)}, f32[256,256]{1,0:T(8,128)S(1)}, f32[128,512]{1,0:T(8,128)S(1)}, f32[136,256]{1,0:T(8,128)S(1)}, f32[1,256]{1,0:T(1,128)S(1)}) custom-call(s32[3]{0:T(128)S(1)} %add_convert_fusion.flags, f32[512,512]{1,0:T(8,128)S(1)} %fusion.1.own, f32[128,512]{1,0:T(8,128)S(1)} %collective-permute-done.other, ...), custom_call_target="tpu_custom_call" | custom-call | flops 629145600 | bytes 2502144 | tf_op jit(solution)/shard_map/pallas_call | solution.py:199
  8.1 2.9 %collective-permute-start.3 = (f32[136,256]{1,0:T(8,128)S(1)}, f32[136,256]{1,0:T(8,128)S(1)}, u32[]{:S(2)}, u32[]{:S(2)}) collective-permute-start(f32[136,256]{1,0:T(8,128)S(1)} %get-tuple-element.29.mine), channel_id=1, source_target_pairs={{0,1},{1,0},{2,3},{3,2},{4,5},{5,4},{6,7},{7,6},{8,9},{9,8},{10,11... | collective-permute-start | bytes 417800 | tf_op jit(solution)/shard_map/ppermute | solution.py:219
  11.0 4.0 %collective-permute-done.3.t = f32[136,256]{1,0:T(8,128)S(1)} collective-permute-done((f32[136,256]{1,0:T(8,128)S(1)}, f32[136,256]{1,0:T(8,128)S(1)}, u32[]{:S(2)}, u32[]{:S(2)}) %collective-permute-start.3) | collective-permute-done | bytes 139296 | tf_op jit(solution)/shard_map/ppermute | solution.py:219
  15.6 1.7 %collective-permute-start.6 = (f32[128,512]{1,0:T(8,128)S(1)}, f32[128,512]{1,0:T(8,128)S(1)}, u32[]{:S(2)}, u32[]{:S(2)}) collective-permute-start(f32[128,512]{1,0:T(8,128)S(1)} %get-tuple-element.35.mine), channel_id=1, source_target_pairs={{0,1},{1,0},{2,3},{3,2},{4,5},{5,4},{6,7},{7,6},{8,9},{9,8},{10,11... | collective-permute-start | bytes 786440 | tf_op jit(solution)/shard_map/ppermute | solution.py:219
  17.3 5.9 %shard_map.60 = (f32[256,256]{1,0:T(8,128)S(1)}, f32[256,256]{1,0:T(8,128)S(1)}, f32[1,256]{1,0:T(1,128)S(1)}) custom-call(s32[3]{0:T(128)S(1)} %add_convert_fusion.flags, f32[136,256]{1,0:T(8,128)S(1)} %get-tuple-element.29.mine, f32[136,256]{1,0:T(8,128)S(1)} %collective-permute-done.2.mine_o, f32[136,256]{1,0:T(8,128)S(1)} %collective-permute-done.3.t, ...), custom_call_target="tpu_custom_call" | custom-call | flops 2013265920 | bytes 1345536 | tf_op jit(solution)/shard_map/pallas_call | solution.py:199
  24.1 4.1 %collective-permute-start.32 = (f32[128]{0:T(128)S(1)}, f32[128]{0:T(128)S(1)}, u32[]{:S(2)}, u32[]{:S(2)}) collective-permute-start(f32[128]{0:T(128)S(1)} %broadcast_select_fusion.14), channel_id=1, source_target_pairs={{0,1},{2,3},{8,9},{10,11},{12,8},{14,10},{16,17},{18,19},{24,25},{... | collective-permute-start | bytes 1544 | tf_op jit(solution)/shard_map/ppermute | solution.py:234
  32.2 1.8 %collective-permute-done.8 = f32[72,256]{1,0:T(8,128)S(1)} collective-permute-done((f32[72,256]{1,0:T(8,128)S(1)}, f32[72,256]{1,0:T(8,128)S(1)}, u32[]{:S(2)}, u32[]{:S(2)}) %collective-permute-start.8) | collective-permute-done | bytes 73760 | tf_op jit(solution)/shard_map/ppermute | solution.py:234
  34.0 2.7 %collective-permute-start.9 = (f32[72,256]{1,0:T(8,128)S(1)}, f32[72,256]{1,0:T(8,128)S(1)}, u32[]{:S(2)}, u32[]{:S(2)}) collective-permute-start(f32[72,256]{1,0:T(8,128)S(1)} %fusion.5.m0), channel_id=1, source_target_pairs={{0,1},{1,0},{2,3},{3,2},{4,5},{5,4},{6,7},{7,6},{8,9},{9,8},{10,11... | collective-permute-start | bytes 221192 | tf_op jit(solution)/shard_map/ppermute | solution.py:219
  36.8 1.7 %collective-permute-start.17 = (f32[72,256]{1,0:T(8,128)S(1)}, f32[72,256]{1,0:T(8,128)S(1)}, u32[]{:S(2)}, u32[]{:S(2)}) collective-permute-start(f32[72,256]{1,0:T(8,128)S(1)} %fusion.5.m0), channel_id=1, source_target_pairs={{0,8},{4,12},{8,0},{12,4},{16,24},{20,28},{24,16},{28,20},{1,9},{5... | collective-permute-start | bytes 221192 | tf_op jit(solution)/shard_map/ppermute | solution.py:219
  42.1 3.5 %collective-permute-done.10.f1 = f32[72,256]{1,0:T(8,128)S(1)} collective-permute-done((f32[72,256]{1,0:T(8,128)S(1)}, f32[72,256]{1,0:T(8,128)S(1)}, u32[]{:S(2)}, u32[]{:S(2)}) %collective-permute-start.10) | collective-permute-done | bytes 73760 | tf_op jit(solution)/shard_map/ppermute | solution.py:219
  45.6 5.0 %collective-permute-start.20 = (f32[128,256]{1,0:T(8,128)S(1)}, f32[128,256]{1,0:T(8,128)S(1)}, u32[]{:S(2)}, u32[]{:S(2)}) collective-permute-start(f32[128,256]{1,0:T(8,128)S(1)} %slice_select_fusion.6), channel_id=1, source_target_pairs={{0,1},{2,3},{8,9},{10,11},{12,8},{14,10},{16,17},{18,19},{24,25},{... | collective-permute-start | bytes 393224 | tf_op jit(solution)/shard_map/ppermute | solution.py:234
  53.9 3.0 %collective-permute-done.21 = f32[64,256]{1,0:T(8,128)S(1)} collective-permute-done((f32[64,256]{1,0:T(8,128)S(1)}, f32[64,256]{1,0:T(8,128)S(1)}, u32[]{:S(2)}, u32[]{:S(2)}) %collective-permute-start.21) | collective-permute-done | bytes 65568 | tf_op jit(solution)/shard_map/ppermute | solution.py:234
  56.9 2.0 %collective-permute-start.19 = (f32[72,256]{1,0:T(8,128)S(1)}, f32[72,256]{1,0:T(8,128)S(1)}, u32[]{:S(2)}, u32[]{:S(2)}) collective-permute-start(f32[72,256]{1,0:T(8,128)S(1)} %collective-permute-done.10.f1), channel_id=1, source_target_pairs={{0,4},{4,0},{8,12},{12,8},{16,20},{20,16},{24,28},{28,24},{1,5},{5... | collective-permute-start | bytes 221192 | tf_op jit(solution)/shard_map/ppermute | solution.py:219
  58.9 1.8 %collective-permute-start.11 = (f32[128,768]{1,0:T(8,128)S(1)}, f32[128,768]{1,0:T(8,128)S(1)}, u32[]{:S(2)}, u32[]{:S(2)}) collective-permute-start(f32[128,768]{1,0:T(8,128)S(1)} %slice_select_fusion.1), channel_id=1, source_target_pairs={{0,1},{2,3},{8,9},{10,11},{12,8},{14,10},{16,17},{18,19},{24,25},{... | collective-permute-start | bytes 1179656 | tf_op jit(solution)/shard_map/ppermute | solution.py:234
  62.0 1.9 %collective-permute-start.26 = (f32[64,768]{1,0:T(8,128)S(1)}, f32[64,768]{1,0:T(8,128)S(1)}, u32[]{:S(2)}, u32[]{:S(2)}) collective-permute-start(f32[64,768]{1,0:T(8,128)S(1)} %select_select_fusion.m0), channel_id=1, source_target_pairs={{0,8},{4,12},{8,0},{12,4},{16,24},{20,28},{24,16},{28,20},{1,9},{5... | collective-permute-start | bytes 589832 | tf_op jit(solution)/shard_map/ppermute | solution.py:219
  63.9 5.4 %shard_map.62 = (f32[256,256]{1,0:T(8,128)S(1)}, f32[256,128]{1,0:T(8,128)S(1)}, f32[256,256]{1,0:T(8,128)S(1)}) custom-call(s32[3]{0:T(128)S(1)} %add_convert_fusion.flags, f32[72,256]{1,0:T(8,128)S(1)} %fusion.5.m0, f32[72,256]{1,0:T(8,128)S(1)} %collective-permute-done.9.m1, f32[72,256]{1,0:T(8,128)S(1)} %collective-permute-done.15.o0, ...), custom_call_target="tpu_custom_call" | custom-call | flops 4026531840 | bytes 1245184 | tf_op jit(solution)/shard_map/pallas_call | solution.py:199
  71.5 5.5 %collective-permute-done.12 = f32[64,768]{1,0:T(8,128)S(1)} collective-permute-done((f32[64,768]{1,0:T(8,128)S(1)}, f32[64,768]{1,0:T(8,128)S(1)}, u32[]{:S(2)}, u32[]{:S(2)}) %collective-permute-start.12) | collective-permute-done | bytes 196640 | tf_op jit(solution)/shard_map/ppermute | solution.py:234
  80.1 2.8 %collective-permute-done.36 = f32[192]{0:T(256)S(1)} collective-permute-done((f32[192]{0:T(256)S(1)}, f32[192]{0:T(256)S(1)}, u32[]{:S(2)}, u32[]{:S(2)}) %collective-permute-start.36) | collective-permute-done | bytes 800 | tf_op jit(solution)/shard_map/ppermute | solution.py:219
  85.0 2.9 %collective-permute-done.38 = f32[768]{0:T(1024)S(1)} collective-permute-done((f32[768]{0:T(1024)S(1)}, f32[768]{0:T(1024)S(1)}, u32[]{:S(2)}, u32[]{:S(2)}) %collective-permute-start.38) | collective-permute-done | bytes 3104 | tf_op jit(solution)/shard_map/ppermute | solution.py:219
  89.2 4.5 %collective-permute-start.41 = (f32[512]{0:T(512)S(1)}, f32[512]{0:T(512)S(1)}, u32[]{:S(2)}, u32[]{:S(2)}) collective-permute-start(f32[512]{0:T(512)S(1)} %pad_maximum_fusion.7), channel_id=1, source_target_pairs={{0,2},{1,3},{4,6},{5,7},{8,10},{9,11},{12,14},{13,15},{16,18},{17,... | collective-permute-start | bytes 6152 | tf_op jit(solution)/shard_map/ppermute | solution.py:213
  93.7 4.5 %collective-permute-start.39 = (f32[256]{0:T(256)S(1)}, f32[256]{0:T(256)S(1)}, u32[]{:S(2)}, u32[]{:S(2)}) collective-permute-start(f32[256]{0:T(256)S(1)} %get-tuple-element.80), channel_id=1, source_target_pairs={{0,16},{4,20},{8,24},{12,28},{1,17},{5,21},{9,25},{13,29},{2,18},{... | collective-permute-start | bytes 3080 | tf_op jit(solution)/shard_map/ppermute | solution.py:213
  100.4 4.1 %collective-permute-done.40 = f32[256]{0:T(256)S(1)} collective-permute-done((f32[256]{0:T(256)S(1)}, f32[256]{0:T(256)S(1)}, u32[]{:S(2)}, u32[]{:S(2)}) %collective-permute-start.40) | collective-permute-done | bytes 1056 | tf_op jit(solution)/shard_map/ppermute | solution.py:213
  105.2 1.8 %collective-permute-done.29.f1 = f32[64,768]{1,0:T(8,128)S(1)} collective-permute-done((f32[64,768]{1,0:T(8,128)S(1)}, f32[64,768]{1,0:T(8,128)S(1)}, u32[]{:S(2)}, u32[]{:S(2)}) %collective-permute-start.29) | collective-permute-done | bytes 196640 | tf_op jit(solution)/shard_map/ppermute | solution.py:219
  108.4 2.4 %shard_map.64 = f32[192,1536]{1,0:T(8,128)} custom-call(s32[3]{0:T(128)S(1)} %add_convert_fusion.flags, f32[192,768]{1,0:T(8,128)S(1)} %fusion.3.re, f32[192,256]{1,0:T(8,128)S(1)} %get-tuple-element.47.g, f32[192,256]{1,0:T(8,128)S(1)} %get-tuple-element.48.gt, f32[64,768]{1,0:T(8,128)S(1)} %select_select_fusion.m0, ...), custom_call_target="tpu_custom_call" | custom-call | flops 452984832 | bytes 3735552 | tf_op jit(solution)/shard_map/pallas_call | solution.py:199
  (131 shorter events, 31.8 us)
Async XLA Ops:
  8.1 6.9 %collective-permute-start.3 = (f32[136,256]{1,0:T(8,128)S(1)}, f32[136,256]{1,0:T(8,128)S(1)}, u32[]{:S(2)}, u32[]{:S(2)}) collective-permute-start(f32[136,256]{1,0:T(8,128)S(1)} %get-tuple-element.29.mine), channel_id=1, source_target_pairs={{0,1},{1,0},{2,3},{3,2},{4,5},{5,4},{6,7},{7,6},{8,9},{9,8},{10,11... | collective-permute-start | bytes 417800 | tf_op jit(solution)/shard_map/ppermute | solution.py:219
  11.0 6.3 %collective-permute-start.2 = (f32[136,256]{1,0:T(8,128)S(1)}, f32[136,256]{1,0:T(8,128)S(1)}, u32[]{:S(2)}, u32[]{:S(2)}) collective-permute-start(f32[136,256]{1,0:T(8,128)S(1)} %get-tuple-element.29.mine), channel_id=1, source_target_pairs={{0,4},{4,0},{8,12},{12,8},{16,20},{20,16},{24,28},{28,24},{1,5},{5... | collective-permute-start | bytes 417800 | tf_op jit(solution)/shard_map/ppermute | solution.py:219
  15.0 14.6 %collective-permute-start.5 = (f32[128,512]{1,0:T(8,128)S(1)}, f32[128,512]{1,0:T(8,128)S(1)}, u32[]{:S(2)}, u32[]{:S(2)}) collective-permute-start(f32[128,512]{1,0:T(8,128)S(1)} %get-tuple-element.35.mine), channel_id=1, source_target_pairs={{0,4},{4,0},{8,12},{12,8},{16,20},{20,16},{24,28},{28,24},{1,5},{5... | collective-permute-start | bytes 786440 | tf_op jit(solution)/shard_map/ppermute | solution.py:219
  15.6 8.4 %collective-permute-start.6 = (f32[128,512]{1,0:T(8,128)S(1)}, f32[128,512]{1,0:T(8,128)S(1)}, u32[]{:S(2)}, u32[]{:S(2)}) collective-permute-start(f32[128,512]{1,0:T(8,128)S(1)} %get-tuple-element.35.mine), channel_id=1, source_target_pairs={{0,1},{1,0},{2,3},{3,2},{4,5},{5,4},{6,7},{7,6},{8,9},{9,8},{10,11... | collective-permute-start | bytes 786440 | tf_op jit(solution)/shard_map/ppermute | solution.py:219
  23.3 6.2 %collective-permute-start.35 = (f32[64]{0:T(128)S(1)}, f32[64]{0:T(128)S(1)}, u32[]{:S(2)}, u32[]{:S(2)}) collective-permute-start(f32[64]{0:T(128)S(1)} %broadcast_select_fusion.7), channel_id=1, source_target_pairs={{1,5},{3,7},{9,13},{11,15},{13,9},{15,11},{17,21},{19,23},{25,29},... | collective-permute-start | bytes 776 | tf_op jit(solution)/shard_map/ppermute | solution.py:234
  24.1 8.1 %collective-permute-start.32 = (f32[128]{0:T(128)S(1)}, f32[128]{0:T(128)S(1)}, u32[]{:S(2)}, u32[]{:S(2)}) collective-permute-start(f32[128]{0:T(128)S(1)} %broadcast_select_fusion.14), channel_id=1, source_target_pairs={{0,1},{2,3},{8,9},{10,11},{12,8},{14,10},{16,17},{18,19},{24,25},{... | collective-permute-start | bytes 1544 | tf_op jit(solution)/shard_map/ppermute | solution.py:234
  28.2 51.0 %collective-permute-start.33 = (f32[64]{0:T(128)S(1)}, f32[64]{0:T(128)S(1)}, u32[]{:S(2)}, u32[]{:S(2)}) collective-permute-start(f32[64]{0:T(128)S(1)} %get-tuple-element.91), channel_id=1, source_target_pairs={{1,0},{3,2},{13,8},{15,10},{17,16},{19,18},{29,24},{31,26}} | collective-permute-start | bytes 776 | tf_op jit(solution)/shard_map/ppermute | solution.py:234
  36.8 17.0 %collective-permute-start.17 = (f32[72,256]{1,0:T(8,128)S(1)}, f32[72,256]{1,0:T(8,128)S(1)}, u32[]{:S(2)}, u32[]{:S(2)}) collective-permute-start(f32[72,256]{1,0:T(8,128)S(1)} %fusion.5.m0), channel_id=1, source_target_pairs={{0,8},{4,12},{8,0},{12,4},{16,24},{20,28},{24,16},{28,20},{1,9},{5... | collective-permute-start | bytes 221192 | tf_op jit(solution)/shard_map/ppermute | solution.py:219
  38.5 20.4 %collective-permute-start.15 = (f32[72,256]{1,0:T(8,128)S(1)}, f32[72,256]{1,0:T(8,128)S(1)}, u32[]{:S(2)}, u32[]{:S(2)}) collective-permute-start(f32[72,256]{1,0:T(8,128)S(1)} %fusion.5.m0), channel_id=1, source_target_pairs={{0,4},{4,0},{8,12},{12,8},{16,20},{20,16},{24,28},{28,24},{1,5},{5... | collective-permute-start | bytes 221192 | tf_op jit(solution)/shard_map/ppermute | solution.py:219
  38.5 12.2 %collective-permute-start.24 = (f32[64,768]{1,0:T(8,128)S(1)}, f32[64,768]{1,0:T(8,128)S(1)}, u32[]{:S(2)}, u32[]{:S(2)}) collective-permute-start(f32[64,768]{1,0:T(8,128)S(1)} %slice_select_fusion.3), channel_id=1, source_target_pairs={{4,0},{5,1},{6,2},{7,3},{8,12},{9,13},{10,14},{11,15},{20,16},{21,... | collective-permute-start | bytes 589832 | tf_op jit(solution)/shard_map/ppermute | solution.py:234
  45.6 7.5 %collective-permute-start.20 = (f32[128,256]{1,0:T(8,128)S(1)}, f32[128,256]{1,0:T(8,128)S(1)}, u32[]{:S(2)}, u32[]{:S(2)}) collective-permute-start(f32[128,256]{1,0:T(8,128)S(1)} %slice_select_fusion.6), channel_id=1, source_target_pairs={{0,1},{2,3},{8,9},{10,11},{12,8},{14,10},{16,17},{18,19},{24,25},{... | collective-permute-start | bytes 393224 | tf_op jit(solution)/shard_map/ppermute | solution.py:234
  50.7 6.2 %collective-permute-start.21 = (f32[64,256]{1,0:T(8,128)S(1)}, f32[64,256]{1,0:T(8,128)S(1)}, u32[]{:S(2)}, u32[]{:S(2)}) collective-permute-start(f32[64,256]{1,0:T(8,128)S(1)} %get-tuple-element.68), channel_id=1, source_target_pairs={{1,0},{3,2},{13,8},{15,10},{17,16},{19,18},{29,24},{31,26}} | collective-permute-start | bytes 196616 | tf_op jit(solution)/shard_map/ppermute | solution.py:234
  53.8 6.9 %collective-permute-start.16 = (f32[72,256]{1,0:T(8,128)S(1)}, f32[72,256]{1,0:T(8,128)S(1)}, u32[]{:S(2)}, u32[]{:S(2)}) collective-permute-start(f32[72,256]{1,0:T(8,128)S(1)} %collective-permute-done.9.m1), channel_id=1, source_target_pairs={{0,4},{4,0},{8,12},{12,8},{16,20},{20,16},{24,28},{28,24},{1,5},{5... | collective-permute-start | bytes 221192 | tf_op jit(solution)/shard_map/ppermute | solution.py:219
  58.9 11.8 %collective-permute-start.11 = (f32[128,768]{1,0:T(8,128)S(1)}, f32[128,768]{1,0:T(8,128)S(1)}, u32[]{:S(2)}, u32[]{:S(2)}) collective-permute-start(f32[128,768]{1,0:T(8,128)S(1)} %slice_select_fusion.1), channel_id=1, source_target_pairs={{0,1},{2,3},{8,9},{10,11},{12,8},{14,10},{16,17},{18,19},{24,25},{... | collective-permute-start | bytes 1179656 | tf_op jit(solution)/shard_map/ppermute | solution.py:234
  60.7 8.6 %collective-permute-start.14 = (f32[64,768]{1,0:T(8,128)S(1)}, f32[64,768]{1,0:T(8,128)S(1)}, u32[]{:S(2)}, u32[]{:S(2)}) collective-permute-start(f32[64,768]{1,0:T(8,128)S(1)} %slice_select_fusion.2), channel_id=1, source_target_pairs={{1,5},{3,7},{9,13},{11,15},{13,9},{15,11},{17,21},{19,23},{25,29},... | collective-permute-start | bytes 589832 | tf_op jit(solution)/shard_map/ppermute | solution.py:234
  61.4 16.5 %collective-permute-start.25 = (f32[64,768]{1,0:T(8,128)S(1)}, f32[64,768]{1,0:T(8,128)S(1)}, u32[]{:S(2)}, u32[]{:S(2)}) collective-permute-start(f32[64,768]{1,0:T(8,128)S(1)} %select_select_fusion.m0), channel_id=1, source_target_pairs={{0,1},{1,0},{2,3},{3,2},{4,5},{5,4},{6,7},{7,6},{8,9},{9,8},{10,11... | collective-permute-start | bytes 589832 | tf_op jit(solution)/shard_map/ppermute | solution.py:219
  62.0 15.9 %collective-permute-start.26 = (f32[64,768]{1,0:T(8,128)S(1)}, f32[64,768]{1,0:T(8,128)S(1)}, u32[]{:S(2)}, u32[]{:S(2)}) collective-permute-start(f32[64,768]{1,0:T(8,128)S(1)} %select_select_fusion.m0), channel_id=1, source_target_pairs={{0,8},{4,12},{8,0},{12,4},{16,24},{20,28},{24,16},{28,20},{1,9},{5... | collective-permute-start | bytes 589832 | tf_op jit(solution)/shard_map/ppermute | solution.py:219
  69.4 7.6 %collective-permute-start.12 = (f32[64,768]{1,0:T(8,128)S(1)}, f32[64,768]{1,0:T(8,128)S(1)}, u32[]{:S(2)}, u32[]{:S(2)}) collective-permute-start(f32[64,768]{1,0:T(8,128)S(1)} %get-tuple-element.63), channel_id=1, source_target_pairs={{1,0},{3,2},{13,8},{15,10},{17,16},{19,18},{29,24},{31,26}} | collective-permute-start | bytes 589832 | tf_op jit(solution)/shard_map/ppermute | solution.py:234
  70.7 7.1 %collective-permute-start.13 = (f32[64,768]{1,0:T(8,128)S(1)}, f32[64,768]{1,0:T(8,128)S(1)}, u32[]{:S(2)}, u32[]{:S(2)}) collective-permute-start(f32[64,768]{1,0:T(8,128)S(1)} %get-tuple-element.62), channel_id=1, source_target_pairs={{1,4},{3,6},{9,12},{11,14},{17,20},{19,22},{25,28},{27,30}} | collective-permute-start | bytes 589832 | tf_op jit(solution)/shard_map/ppermute | solution.py:234
  87.9 16.7 %collective-permute-start.42 = (f32[512]{0:T(512)S(1)}, f32[512]{0:T(512)S(1)}, u32[]{:S(2)}, u32[]{:S(2)}) collective-permute-start(f32[512]{0:T(512)S(1)} %pad_maximum_fusion.8), channel_id=1, source_target_pairs={{2,0},{3,1},{6,4},{7,5},{10,8},{11,9},{14,12},{15,13},{18,16},{19,... | collective-permute-start | bytes 6152 | tf_op jit(solution)/shard_map/ppermute | solution.py:213
  89.2 15.9 %collective-permute-start.41 = (f32[512]{0:T(512)S(1)}, f32[512]{0:T(512)S(1)}, u32[]{:S(2)}, u32[]{:S(2)}) collective-permute-start(f32[512]{0:T(512)S(1)} %pad_maximum_fusion.7), channel_id=1, source_target_pairs={{0,2},{1,3},{4,6},{5,7},{8,10},{9,11},{12,14},{13,15},{16,18},{17,... | collective-permute-start | bytes 6152 | tf_op jit(solution)/shard_map/ppermute | solution.py:213
  98.2 6.4 %collective-permute-start.40 = (f32[256]{0:T(256)S(1)}, f32[256]{0:T(256)S(1)}, u32[]{:S(2)}, u32[]{:S(2)}) collective-permute-start(f32[256]{0:T(256)S(1)} %get-tuple-element.77), channel_id=1, source_target_pairs={{16,0},{20,4},{24,8},{28,12},{17,1},{21,5},{25,9},{29,13},{18,2},{... | collective-permute-start | bytes 3080 | tf_op jit(solution)/shard_map/ppermute | solution.py:213
  99.5 7.4 %collective-permute-start.27 = (f32[64,768]{1,0:T(8,128)S(1)}, f32[64,768]{1,0:T(8,128)S(1)}, u32[]{:S(2)}, u32[]{:S(2)}) collective-permute-start(f32[64,768]{1,0:T(8,128)S(1)} %select_select_fusion.m0), channel_id=1, source_target_pairs={{0,4},{4,0},{8,12},{12,8},{16,20},{20,16},{24,28},{28,24},{1,5},{5... | collective-permute-start | bytes 589832 | tf_op jit(solution)/shard_map/ppermute | solution.py:219
  99.6 7.3 %collective-permute-start.29 = (f32[64,768]{1,0:T(8,128)S(1)}, f32[64,768]{1,0:T(8,128)S(1)}, u32[]{:S(2)}, u32[]{:S(2)}) collective-permute-start(f32[64,768]{1,0:T(8,128)S(1)} %collective-permute-done.25.m1), channel_id=1, source_target_pairs={{0,8},{4,12},{8,0},{12,4},{16,24},{20,28},{24,16},{28,20},{1,9},{5... | collective-permute-start | bytes 589832 | tf_op jit(solution)/shard_map/ppermute | solution.py:219
  (22 other events, 64.4 us)

commit v2 on v1

--- a/solution.py
+++ b/solution.py
@@ -138,7 +138,7 @@
     h_out[...] = h[...] - change
 
 
-def apply2(flags, re, g, gt, mine, mine_o, t, t_o, ext, inner):
+def apply2(flags, re, g, gt, mine, mine_o, t, t_o, ext):
     left, low, first = flags[0] == 1, flags[1] == 1, flags[2] == 1
     s = mine.shape[0]
     own = re[...] + dot3(gt[...], ordered(left, mine[...], mine_o[...]))
@@ -149,45 +149,48 @@
     east = jnp.concatenate([lows[:, s : 2 * s], ups[:, s : 2 * s]], axis=1)
     ext[:, : 2 * s] = jnp.where(first, west, east)
     ext[:, 2 * s : 4 * s] = lows[:, 2 * s :]
-    ext[:, 4 * s :] = ups[:, 2 * s :]
-    inner[...] = jnp.where(first, east, west)
-
-
-def quads(flags, mine, other):
+    ext[:, 4 * s : 6 * s] = ups[:, 2 * s :]
+    ext[:, 6 * s :] = jnp.where(first, east, west)
+
+
+def quads(flags, v, beside, far, far_beside, near, last, part):
     left, low = flags[0] == 1, flags[1] == 1
-    a = ordered(left, mine[0], other[0])
-    b = ordered(left, mine[1], other[1])
-    return ordered(low, a, b)
-
-
-def solve3(flags, m0, m1, o0, o1, f0, f1, p0, p1, inverse, jump, t_out):
-    low = flags[1] == 1
-    n = m0.shape[0] - 8
-
-    def both(a, b):
-        rows = quads(flags, [r[0:n, :] for r in a], [r[0:n, :] for r in b])
-        h0, h1 = a[0][n : n + 1, 0 : 2 * n], a[1][n : n + 1, 0 : 2 * n]
-        vec = jnp.concatenate(
-            [jnp.where(low, h0, h1), jnp.where(low, h1, h0)], axis=1
+    n = v.shape[0]
+    other = [near[0:n], near[n : 2 * n], near[2 * n : 3 * n], last[...]]
+    a, b, c, d = [
+        part(left, mine, theirs)
+        for mine, theirs in zip((v[...], beside[...], far[...], far_beside[...]), other)
+    ]
+    axis = 0 if a.shape[0] > 1 else 1
+
+    def stack(one, two):
+        return jnp.concatenate(
+            [jnp.where(low, one, two), jnp.where(low, two, one)], axis=axis
         )
-        return rows, vec
-
-    o_ii, o_h = both((m0, m1), (o0, o1))
-    t_ii, t_h = both((f0, f1), (p0, p1))
-    inverse[...], jump[...] = interface(t_ii, o_ii, t_h, o_h)
-    t_out[...] = t_ii
-
-
-def gain3(flags, inverse, jump, t_ii, ri, g, gt, change):
-    g[...], gt[...], change[...] = apply_gain(inverse[...], jump[...], t_ii[...], ri[...])
-
-
-def apply3(scale, flags, re, g, gt, m0, m1, o0, o1, f0, f1, p0, p1, out):
+
+    return stack(a, b), stack(c, d)
+
+
+def gain3(flags, v, beside, far, far_beside, near, last, rows, g, gt, change):
+    n = v.shape[0] - 8
+    e = 12 * n
+    pieces = (v, beside, far, far_beside, near, last)
+    o_ii, t_ii = quads(
+        flags, *pieces, lambda left, a, b: ordered(left, a[0:n, e:], b[0:n, e:])
+    )
+    o_h, t_h = quads(flags, *pieces, lambda left, a, b: a[n : n + 1, 0 : 2 * n])
+    g[...], gt[...], change[...] = gain(t_ii, o_ii, rows[:, e:], t_h, o_h)
+
+
+def apply3(scale, flags, v, beside, far, far_beside, near, last, rows, g, gt, out):
     first = flags[2] == 1
-    e = re.shape[1]
-    o_ie = quads(flags, (m0[...], m1[...]), (o0[...], o1[...]))
-    t_ie = quads(flags, (f0[...], f1[...]), (p0[...], p1[...]))
-    own = (re[...] + dot3(gt[...], o_ie)) * scale
+    n = v.shape[0] - 8
+    e = 12 * n
+    pieces = (v, beside, far, far_beside, near, last)
+    o_ie, t_ie = quads(
+        flags, *pieces, lambda left, a, b: ordered(left, a[0:n, :e], b[0:n, :e])
+    )
+    own = (rows[:, :e] + dot3(gt[...], o_ie)) * scale
     cross = dot3(g[...], t_ie) * (-scale)
     out[:, :e] = jnp.where(first, own, cross)
     out[:, e:] = jnp.where(first, cross, own)
@@ -281,39 +284,34 @@
         [(2 * s, 2 * s), (2 * s, 2 * s), (1, 2 * s)],
         6 * (2 * s) ** 3 * 20,
     )
-    ext, inner = call(
+    (merged,) = call(
         apply2,
         flags,
         [re, g, gt, ie, ie_o, t_ie, t_ie_o],
-        [(2 * s, 6 * s), (2 * s, 2 * s)],
+        [(2 * s, 8 * s)],
         6 * (2 * s) ** 2 * 8 * s,
     )
 
     half = s // 2
-    x_i, x_e = inner[:s], ext[:s]
-    to_first = lambda a: jnp.where(left, a[half:], a[:half])
-    keep = lambda a: jnp.where(left, a[:half], a[half:])
+    x, y, h_x, h_y = merged[:s], merged[s:], h[:, :s], h[:, s:]
+
+    def pack(rows, vector):
+        row = jnp.pad(vector, ((0, 0), (0, 7 * s)))
+        return jnp.concatenate([rows, jnp.broadcast_to(row, (8, 8 * s))], axis=0)
+
     holder = left != first
 
     def give(i, j):
         return (i ^ 1, j) if (i % 2 == 0) != (i // 2 % 2 == 0) else None
 
-    h_x = jnp.broadcast_to(jnp.concatenate([h[:, :s], h[:, :s]], axis=1), (8, 2 * s))
-    got_i = send(jnp.concatenate([to_first(x_i), h_x], axis=0), give)
-    got_e = send(after(to_first(x_e), got_i), give)
-    v_i = jnp.where(holder, jnp.concatenate([keep(x_i), h_x], axis=0), got_i)
-    v_e = jnp.where(holder, keep(x_e), got_e)
-
-    def spread_out(v):
-        beside = partner(v, "gy", 0)
-        far = partner(v, "gx", 1)
-        far_beside = partner(beside, "gx", 1)
-        pieces = [v, beside, far, far_beside]
-        shared = [partner(piece, "gx", 0) for piece in pieces]
-        return pieces[:2] + shared[:2] + pieces[2:] + shared[2:]
-
-    quad_i = spread_out(v_i)
-    quad_e = spread_out(after(v_e, quad_i[5]))
+    got = send(pack(jnp.where(left, x[half:], x[:half]), h_x), give)
+    v = jnp.where(holder, pack(jnp.where(left, x[:half], x[half:]), h_x), got)
+    beside = partner(v, "gy", 0)
+    far = partner(v, "gx", 1)
+    far_beside = partner(beside, "gx", 1)
+    near = partner(jnp.concatenate([v, beside, far], axis=0), "gx", 0)
+    last = partner(far_beside, "gx", 0)
+    pieces = [v, beside, far, far_beside, near, last]
 
     def in_first(i):
         return i // 2 % 2 == 0
@@ -338,49 +336,49 @@
             return (i ^ 1, j)
         return None
 
-    def rows_of(a):
-        x, y = a[:s], a[s:]
-        got_a = send(jnp.where(left, y, x), move_a)
-        got_b = send(x[:half], move_b)
-        got_c = send(y[:half], move_c)
-        got_d = send(jnp.where(left, y[half:], x[half:]), move_d)
+    got_a = send(jnp.where(left, pack(y, h_y), pack(x, h_x)), move_a)
+    got_b = send(pack(x[:half], h_x), move_b)
+    got_c = send(pack(y[:half], h_y), move_c)
+    got_d = send(
+        jnp.where(left, pack(y[half:], h_y), pack(x[half:], h_x)), move_d
+    )
+
+    def assemble(x, y, a, b, c, d):
         lower = jnp.where(
             left,
-            jnp.concatenate([jnp.where(first, x, got_a), got_b], axis=0),
-            jnp.concatenate([y, got_c], axis=0),
+            jnp.concatenate([jnp.where(first, x, a), b], axis=0),
+            jnp.concatenate([y, c], axis=0),
         )
         upper = jnp.where(
             left,
-            jnp.concatenate([jnp.where(first, x[half:], got_d), got_a], axis=0),
-            jnp.concatenate([got_d, y], axis=0),
+            jnp.concatenate([jnp.where(first, x[half:], d), a], axis=0),
+            jnp.concatenate([d, y], axis=0),
         )
         return jnp.where(low, lower, upper)
 
-    row_i = rows_of(after(inner, quad_i[1]))
-    row_h = rows_of(h[0])
-    row_e = rows_of(after(ext, quad_i[5]))
+    rows = assemble(x, y, got_a[:s], got_b[:half], got_c[:half], got_d[:half])
+    row_h = assemble(
+        h_x[0],
+        h_y[0],
+        got_a[s, :s],
+        got_b[half, :half],
+        got_c[half, :half],
+        got_d[half, half:s],
+    )
     rows_dev = 3 * s // 2
-    solved = call(
-        solve3,
-        flags,
-        quad_i,
-        [(2 * s, 2 * s), (2 * s, 128), (2 * s, 2 * s)],
-        6 * (2 * s) ** 3 * 40,
-    )
-    row_i = after(row_i, (quad_e[1], quad_e[4], row_e))
     g, gt, change = call(
         gain3,
         flags,
-        [*solved, row_i],
+        [*pieces, rows],
         [(rows_dev, 2 * s), (rows_dev, 2 * s), (1, 2 * s)],
-        6 * (2 * s) ** 3 * 2,
+        6 * (2 * s) ** 3 * 20,
     )
     h3 = row_h - change[0, :rows_dev]
     scale = math.sqrt(12 * s)
     (scaled,) = call(
         functools.partial(apply3, scale),
         flags,
-        [row_e, g, gt, *quad_e],
+        [*pieces, rows, g, gt],
         [(rows_dev, 12 * s)],
         6 * rows_dev * 2 * s * 12 * s,
     )

time: 113 us -> 102 us (0.903)
  starting transfers between devices: 53 us -> 30.2 us
  waiting for transfers between devices: 33.7 us -> 41.5 us
  local copies, waits for them, and re-layouts: 0.26 us -> 3.25 us
  other arithmetic: 4.68 us -> 6.15 us
    ppermute x25 -> x16, waiting for transfers between devices: 18.2 us -> 39.7 us  [partner(): return lax.ppermute(value, axis, pairs)]
    ppermute x14 -> x5, starting transfers between devices: 21.5 us -> 9.05 us  [send(): return lax.ppermute(value, ('gx', 'gy'), pairs)]
    ppermute x14 -> x5, waiting for transfers between devices: 11.4 us -> 0.1 us  [send(): return lax.ppermute(value, ('gx', 'gy'), pairs)]
    ppermute x25 -> x16, starting transfers between devices: 19.8 us -> 10.7 us  [partner(): return lax.ppermute(value, axis, pairs)]
    concatenate x1 -> x5, local copies, waits for them, and re-layouts: 0.01 us -> 2.77 us  [the longest x2 1.07 us: assemble(): jnp.concatenate([y, c], axis=0)]
    ppermute x4, waiting for transfers between devices: 4.15 us -> 1.72 us  [from_behind(): return lax.ppermute(block, axis, route)]
    pallas_call x6 -> x5, Pallas kernels: 19.9 us -> 19.1 us  [call(): pl.pallas_call(body, out_shape=outs, in_specs=[pl.BlockSpec(memory_space=...]
  transfers between devices with their start and end apart: 43 -> 25, of which waited for: 13 -> 12; matrix products, arithmetic and copies ran while one was open for 1% -> 4% of each run, Pallas kernels for 12% -> 8%
where the time goes in v2:
time: 102 us; the launch traced here: 101 us
  waiting for transfers between devices  41.5 us (41%)
  starting transfers between devices  30.2 us (30%)
  Pallas kernels  19.1 us (19%)
  other arithmetic  6.15 us (6%)
  local copies, waits for them, and re-layouts  3.25 us (3%)
  between operations  1.2 us (1%)
    ppermute x16, waiting for transfers between devices, partner(): return lax.ppermute(value, axis, pairs)  39.7 us
    pallas_call x5, Pallas kernels, call(): pl.pallas_call(body, out_shape=outs, in_specs=[pl.BlockSpec(memory_space=...  19.1 us
    ppermute x16, starting transfers between devices, partner(): return lax.ppermute(value, axis, pairs)  10.7 us
    ppermute x4, starting transfers between devices, from_behind(): return lax.ppermute(block, axis, route)  10.5 us
    ppermute x5, starting transfers between devices, send(): return lax.ppermute(value, ('gx', 'gy'), pairs)  9.05 us
  transfers between devices with their start and end apart: 25, of which 12 were waited for; matrix products, arithmetic and copies ran while one was open for 4% of the time, Pallas kernels for 8%

profile of v2, /device:TPU:0, one launch (start us, length us, event | category | flops | bytes accessed | tf_op | source)
XLA Modules:
  0.0 101.4 jit_solution(16799930773260099510)
XLA Ops:
  4.3 3.8 %shard_map.59 = (f32[256,512]{1,0:T(8,128)S(1)}, f32[256,256]{1,0:T(8,128)S(1)}, f32[128,512]{1,0:T(8,128)S(1)}, f32[136,256]{1,0:T(8,128)S(1)}, f32[1,256]{1,0:T(1,128)S(1)}) custom-call(s32[3]{0:T(128)S(1)} %add_convert_fusion.flags, f32[512,512]{1,0:T(8,128)S(1)} %fusion.1.own, f32[128,512]{1,0:T(8,128)S(1)} %collective-permute-done.other, ...), custom_call_target="tpu_custom_call" | custom-call | flops 629145600 | bytes 2502144 | tf_op jit(solution)/shard_map/pallas_call | solution.py:202
  8.1 2.9 %collective-permute-start.3 = (f32[136,256]{1,0:T(8,128)S(1)}, f32[136,256]{1,0:T(8,128)S(1)}, u32[]{:S(2)}, u32[]{:S(2)}) collective-permute-start(f32[136,256]{1,0:T(8,128)S(1)} %get-tuple-element.19.mine), channel_id=1, source_target_pairs={{0,1},{1,0},{2,3},{3,2},{4,5},{5,4},{6,7},{7,6},{8,9},{9,8},{10,11... | collective-permute-start | bytes 417800 | tf_op jit(solution)/shard_map/ppermute | solution.py:222
  11.0 4.0 %collective-permute-done.3.t = f32[136,256]{1,0:T(8,128)S(1)} collective-permute-done((f32[136,256]{1,0:T(8,128)S(1)}, f32[136,256]{1,0:T(8,128)S(1)}, u32[]{:S(2)}, u32[]{:S(2)}) %collective-permute-start.3) | collective-permute-done | bytes 139296 | tf_op jit(solution)/shard_map/ppermute | solution.py:222
  15.0 1.7 %collective-permute-start.6 = (f32[128,512]{1,0:T(8,128)S(1)}, f32[128,512]{1,0:T(8,128)S(1)}, u32[]{:S(2)}, u32[]{:S(2)}) collective-permute-start(f32[128,512]{1,0:T(8,128)S(1)} %get-tuple-element.25.mine), channel_id=1, source_target_pairs={{0,1},{1,0},{2,3},{3,2},{4,5},{5,4},{6,7},{7,6},{8,9},{9,8},{10,11... | collective-permute-start | bytes 786440 | tf_op jit(solution)/shard_map/ppermute | solution.py:222
  17.3 5.7 %collective-permute-done.6.t = f32[128,512]{1,0:T(8,128)S(1)} collective-permute-done((f32[128,512]{1,0:T(8,128)S(1)}, f32[128,512]{1,0:T(8,128)S(1)}, u32[]{:S(2)}, u32[]{:S(2)}) %collective-permute-start.6) | collective-permute-done | bytes 262176 | tf_op jit(solution)/shard_map/ppermute | solution.py:222
  22.9 5.9 %shard_map.60 = (f32[256,256]{1,0:T(8,128)S(1)}, f32[256,256]{1,0:T(8,128)S(1)}, f32[1,256]{1,0:T(1,128)S(1)}) custom-call(s32[3]{0:T(128)S(1)} %add_convert_fusion.flags, f32[136,256]{1,0:T(8,128)S(1)} %get-tuple-element.19.mine, f32[136,256]{1,0:T(8,128)S(1)} %collective-permute-done.2.mine_o, f32[136,256]{1,0:T(8,128)S(1)} %collective-permute-done.3.t, ...), custom_call_target="tpu_custom_call" | custom-call | flops 2013265920 | bytes 1345536 | tf_op jit(solution)/shard_map/pallas_call | solution.py:202
  31.7 5.1 %collective-permute-start.14 = (f32[136,1024]{1,0:T(8,128)S(1)}, f32[136,1024]{1,0:T(8,128)S(1)}, u32[]{:S(2)}, u32[]{:S(2)}) collective-permute-start(f32[136,1024]{1,0:T(8,128)S(1)} %maximum_select_fusion.2), channel_id=1, source_target_pairs={{0,1},{2,3},{8,9},{10,11},{12,8},{14,10},{16,17},{18,19},{24,25},{... | collective-permute-start | bytes 1671176 | tf_op jit(solution)/shard_map/ppermute | solution.py:237
  37.0 1.3 %collective-permute-start.8 = (f32[72,1024]{1,0:T(8,128)S(1)}, f32[72,1024]{1,0:T(8,128)S(1)}, u32[]{:S(2)}, u32[]{:S(2)}) collective-permute-start(f32[72,1024]{1,0:T(8,128)S(1)} %get-tuple-element.62), channel_id=1, source_target_pairs={{4,0},{5,1},{6,2},{7,3},{8,12},{9,13},{10,14},{11,15},{20,16},{21,... | collective-permute-start | bytes 884744 | tf_op jit(solution)/shard_map/ppermute | solution.py:237
  39.1 1.3 %collective-permute-start.15 = (f32[72,1024]{1,0:T(8,128)S(1)}, f32[72,1024]{1,0:T(8,128)S(1)}, u32[]{:S(2)}, u32[]{:S(2)}) collective-permute-start(f32[72,1024]{1,0:T(8,128)S(1)} %get-tuple-element.61), channel_id=1, source_target_pairs={{1,0},{3,2},{13,8},{15,10},{17,16},{19,18},{29,24},{31,26}} | collective-permute-start | bytes 884744 | tf_op jit(solution)/shard_map/ppermute | solution.py:237
  40.6 1.5 %collective-permute-start.10 = (f32[72,1024]{1,0:T(8,128)S(1)}, f32[72,1024]{1,0:T(8,128)S(1)}, u32[]{:S(2)}, u32[]{:S(2)}) collective-permute-start(f32[72,1024]{1,0:T(8,128)S(1)} %fusion.5.v), channel_id=1, source_target_pairs={{0,8},{4,12},{8,0},{12,4},{16,24},{20,28},{24,16},{28,20},{1,9},{5... | collective-permute-start | bytes 884744 | tf_op jit(solution)/shard_map/ppermute | solution.py:222
  42.1 2.6 %collective-permute-start.9 = (f32[72,1024]{1,0:T(8,128)S(1)}, f32[72,1024]{1,0:T(8,128)S(1)}, u32[]{:S(2)}, u32[]{:S(2)}) collective-permute-start(f32[72,1024]{1,0:T(8,128)S(1)} %fusion.5.v), channel_id=1, source_target_pairs={{0,1},{1,0},{2,3},{3,2},{4,5},{5,4},{6,7},{7,6},{8,9},{9,8},{10,11... | collective-permute-start | bytes 884744 | tf_op jit(solution)/shard_map/ppermute | solution.py:222
  45.4 5.0 %collective-permute-done.10.far = f32[72,1024]{1,0:T(8,128)S(1)} collective-permute-done((f32[72,1024]{1,0:T(8,128)S(1)}, f32[72,1024]{1,0:T(8,128)S(1)}, u32[]{:S(2)}, u32[]{:S(2)}) %collective-permute-start.10) | collective-permute-done | bytes 294944 | tf_op jit(solution)/shard_map/ppermute | solution.py:222
  50.4 6.8 %collective-permute-done.9.beside = f32[72,1024]{1,0:T(8,128)S(1)} collective-permute-done((f32[72,1024]{1,0:T(8,128)S(1)}, f32[72,1024]{1,0:T(8,128)S(1)}, u32[]{:S(2)}, u32[]{:S(2)}) %collective-permute-start.9) | collective-permute-done | bytes 294944 | tf_op jit(solution)/shard_map/ppermute | solution.py:222
  58.5 8.3 %collective-permute-done.11.far_beside = f32[72,1024]{1,0:T(8,128)S(1)} collective-permute-done((f32[72,1024]{1,0:T(8,128)S(1)}, f32[72,1024]{1,0:T(8,128)S(1)}, u32[]{:S(2)}, u32[]{:S(2)}) %collective-permute-start.11) | collective-permute-done | bytes 294944 | tf_op jit(solution)/shard_map/ppermute | solution.py:222
  68.4 5.9 %shard_map.62 = (f32[192,256]{1,0:T(8,128)S(1)}, f32[192,256]{1,0:T(8,128)S(1)}, f32[1,256]{1,0:T(1,128)S(1)}) custom-call(s32[3]{0:T(128)S(1)} %add_convert_fusion.flags, f32[72,1024]{1,0:T(8,128)S(1)} %fusion.5.v, f32[72,1024]{1,0:T(8,128)S(1)} %collective-permute-done.9.beside, f32[72,1024]{1,0:T(8,128)S(1)} %collective-permute-done.10.far, ...), custom_call_target="tpu_custom_call" | custom-call | flops 2013265920 | bytes 3539968 | tf_op jit(solution)/shard_map/pallas_call | solution.py:202
  74.4 3.6 %collective-permute-done.18 = f32[192]{0:T(256)S(1)} collective-permute-done((f32[192]{0:T(256)S(1)}, f32[192]{0:T(256)S(1)}, u32[]{:S(2)}, u32[]{:S(2)}) %collective-permute-start.18) | collective-permute-done | bytes 800 | tf_op jit(solution)/shard_map/ppermute | solution.py:222
  80.1 3.7 %collective-permute-done.20 = f32[768]{0:T(1024)} collective-permute-done((f32[768]{0:T(1024)}, f32[768]{0:T(1024)}, u32[]{:S(2)}, u32[]{:S(2)}) %collective-permute-start.20) | collective-permute-done | bytes 3104 | tf_op jit(solution)/shard_map/ppermute | solution.py:222
  84.5 4.5 %collective-permute-start.21 = (f32[256]{0:T(256)S(1)}, f32[256]{0:T(256)S(1)}, u32[]{:S(2)}, u32[]{:S(2)}) collective-permute-start(f32[256]{0:T(256)S(1)} %get-tuple-element.70), channel_id=1, source_target_pairs={{0,16},{4,20},{8,24},{12,28},{1,17},{5,21},{9,25},{13,29},{2,18},{... | collective-permute-start | bytes 3080 | tf_op jit(solution)/shard_map/ppermute | solution.py:216
  89.0 1.3 %collective-permute-start.22 = (f32[256]{0:T(256)S(1)}, f32[256]{0:T(256)S(1)}, u32[]{:S(2)}, u32[]{:S(2)}) collective-permute-start(f32[256]{0:T(256)S(1)} %get-tuple-element.67), channel_id=1, source_target_pairs={{16,0},{20,4},{24,8},{28,12},{17,1},{21,5},{25,9},{29,13},{18,2},{... | collective-permute-start | bytes 3080 | tf_op jit(solution)/shard_map/ppermute | solution.py:216
  90.3 3.4 %collective-permute-start.23 = (f32[512]{0:T(512)S(1)}, f32[512]{0:T(512)S(1)}, u32[]{:S(2)}, u32[]{:S(2)}) collective-permute-start(f32[512]{0:T(512)S(1)} %pad_maximum_fusion.12), channel_id=1, source_target_pairs={{0,2},{1,3},{4,6},{5,7},{8,10},{9,11},{12,14},{13,15},{16,18},{17,... | collective-permute-start | bytes 6152 | tf_op jit(solution)/shard_map/ppermute | solution.py:216
  93.7 1.3 %collective-permute-start.24 = (f32[512]{0:T(512)S(1)}, f32[512]{0:T(512)S(1)}, u32[]{:S(2)}, u32[]{:S(2)}) collective-permute-start(f32[512]{0:T(512)S(1)} %pad_maximum_fusion.13), channel_id=1, source_target_pairs={{2,0},{3,1},{6,4},{7,5},{10,8},{11,9},{14,12},{15,13},{18,16},{19,... | collective-permute-start | bytes 6152 | tf_op jit(solution)/shard_map/ppermute | solution.py:216
  95.0 2.4 %shard_map.63 = f32[192,1536]{1,0:T(8,128)} custom-call(s32[3]{0:T(128)S(1)} %add_convert_fusion.flags, f32[72,1024]{1,0:T(8,128)S(1)} %fusion.5.v, f32[72,1024]{1,0:T(8,128)S(1)} %collective-permute-done.9.beside, f32[72,1024]{1,0:T(8,128)S(1)} %collective-permute-done.10.far, f32[72,1024]{1,0:T(8,128)S(1)} %collective-permute-done.11.far_beside, ...), custom_call_target="tpu_custom_call" | custom-call | flops 452984832 | bytes 4718592 | tf_op jit(solution)/shard_map/pallas_call | solution.py:202
  97.5 1.7 %collective-permute-done.24 = f32[512]{0:T(512)S(1)} collective-permute-done((f32[512]{0:T(512)S(1)}, f32[512]{0:T(512)S(1)}, u32[]{:S(2)}, u32[]{:S(2)}) %collective-permute-start.24) | collective-permute-done | bytes 2080 | tf_op jit(solution)/shard_map/ppermute | solution.py:216
  99.3 1.4 %multiply_reduce_fusion = f32[192]{0:T(256)S(1)} fusion(f32[192,1536]{1,0:T(8,128)} %shard_map.63, f32[1536]{0:T(1024)S(1)} %negate_multiply_fusion), kind=kLoop, calls=%fused_computation.2 | loop fusion | flops 589632 | bytes 1186560 | tf_op jit(solution)/shard_map/reduce_sum | solution.py:408
  (115 shorter events, 15.3 us)
Async XLA Ops:
  2.2 2.2 %collective-permute-start = (f32[128,512]{1,0:T(8,128)S(1)}, f32[128,512]{1,0:T(8,128)S(1)}, u32[]{:S(2)}, u32[]{:S(2)}) collective-permute-start(f32[128,512]{1,0:T(8,128)S(1)} %slice.140), channel_id=1, source_target_pairs={{0,4},{4,0},{8,12},{12,8},{16,20},{20,16},{24,28},{28,24},{1,5},{5... | collective-permute-start | bytes 786440 | tf_op jit(solution)/shard_map/ppermute | solution.py:222
  3.0 1.3 %collective-permute-start.1 = (f32[1,128]{1,0:T(1,128)S(1)}, f32[1,128]{1,0:T(1,128)S(1)}, u32[]{:S(2)}, u32[]{:S(2)}) collective-permute-start(f32[1,128]{1,0:T(1,128)S(1)} %slice.141), channel_id=1, source_target_pairs={{0,4},{4,0},{8,12},{12,8},{16,20},{20,16},{24,28},{28,24},{1,5},{5... | collective-permute-start | bytes 1544 | tf_op jit(solution)/shard_map/ppermute | solution.py:222
  8.1 6.9 %collective-permute-start.3 = (f32[136,256]{1,0:T(8,128)S(1)}, f32[136,256]{1,0:T(8,128)S(1)}, u32[]{:S(2)}, u32[]{:S(2)}) collective-permute-start(f32[136,256]{1,0:T(8,128)S(1)} %get-tuple-element.19.mine), channel_id=1, source_target_pairs={{0,1},{1,0},{2,3},{3,2},{4,5},{5,4},{6,7},{7,6},{8,9},{9,8},{10,11... | collective-permute-start | bytes 417800 | tf_op jit(solution)/shard_map/ppermute | solution.py:222
  15.0 7.9 %collective-permute-start.6 = (f32[128,512]{1,0:T(8,128)S(1)}, f32[128,512]{1,0:T(8,128)S(1)}, u32[]{:S(2)}, u32[]{:S(2)}) collective-permute-start(f32[128,512]{1,0:T(8,128)S(1)} %get-tuple-element.25.mine), channel_id=1, source_target_pairs={{0,1},{1,0},{2,3},{3,2},{4,5},{5,4},{6,7},{7,6},{8,9},{9,8},{10,11... | collective-permute-start | bytes 786440 | tf_op jit(solution)/shard_map/ppermute | solution.py:222
  16.8 6.2 %collective-permute-start.2 = (f32[136,256]{1,0:T(8,128)S(1)}, f32[136,256]{1,0:T(8,128)S(1)}, u32[]{:S(2)}, u32[]{:S(2)}) collective-permute-start(f32[136,256]{1,0:T(8,128)S(1)} %get-tuple-element.19.mine), channel_id=1, source_target_pairs={{0,4},{4,0},{8,12},{12,8},{16,20},{20,16},{24,28},{28,24},{1,5},{5... | collective-permute-start | bytes 417800 | tf_op jit(solution)/shard_map/ppermute | solution.py:222
  16.8 6.2 %collective-permute-start.4 = (f32[136,256]{1,0:T(8,128)S(1)}, f32[136,256]{1,0:T(8,128)S(1)}, u32[]{:S(2)}, u32[]{:S(2)}) collective-permute-start(f32[136,256]{1,0:T(8,128)S(1)} %collective-permute-done.3.t), channel_id=1, source_target_pairs={{0,4},{4,0},{8,12},{12,8},{16,20},{20,16},{24,28},{28,24},{1,5},{5... | collective-permute-start | bytes 417800 | tf_op jit(solution)/shard_map/ppermute | solution.py:222
  17.3 12.2 %collective-permute-start.5 = (f32[128,512]{1,0:T(8,128)S(1)}, f32[128,512]{1,0:T(8,128)S(1)}, u32[]{:S(2)}, u32[]{:S(2)}) collective-permute-start(f32[128,512]{1,0:T(8,128)S(1)} %get-tuple-element.25.mine), channel_id=1, source_target_pairs={{0,4},{4,0},{8,12},{12,8},{16,20},{20,16},{24,28},{28,24},{1,5},{5... | collective-permute-start | bytes 786440 | tf_op jit(solution)/shard_map/ppermute | solution.py:222
  22.9 6.5 %collective-permute-start.7 = (f32[128,512]{1,0:T(8,128)S(1)}, f32[128,512]{1,0:T(8,128)S(1)}, u32[]{:S(2)}, u32[]{:S(2)}) collective-permute-start(f32[128,512]{1,0:T(8,128)S(1)} %collective-permute-done.6.t), channel_id=1, source_target_pairs={{0,4},{4,0},{8,12},{12,8},{16,20},{20,16},{24,28},{28,24},{1,5},{5... | collective-permute-start | bytes 786440 | tf_op jit(solution)/shard_map/ppermute | solution.py:222
  30.8 6.0 %collective-permute-start.17 = (f32[72,1024]{1,0:T(8,128)S(1)}, f32[72,1024]{1,0:T(8,128)S(1)}, u32[]{:S(2)}, u32[]{:S(2)}) collective-permute-start(f32[72,1024]{1,0:T(8,128)S(1)} %fusion.4), channel_id=1, source_target_pairs={{1,5},{3,7},{9,13},{11,15},{13,9},{15,11},{17,21},{19,23},{25,29},... | collective-permute-start | bytes 884744 | tf_op jit(solution)/shard_map/ppermute | solution.py:237
  31.7 13.6 %collective-permute-start.14 = (f32[136,1024]{1,0:T(8,128)S(1)}, f32[136,1024]{1,0:T(8,128)S(1)}, u32[]{:S(2)}, u32[]{:S(2)}) collective-permute-start(f32[136,1024]{1,0:T(8,128)S(1)} %maximum_select_fusion.2), channel_id=1, source_target_pairs={{0,1},{2,3},{8,9},{10,11},{12,8},{14,10},{16,17},{18,19},{24,25},{... | collective-permute-start | bytes 1671176 | tf_op jit(solution)/shard_map/ppermute | solution.py:237
  37.0 3.5 %collective-permute-start.8 = (f32[72,1024]{1,0:T(8,128)S(1)}, f32[72,1024]{1,0:T(8,128)S(1)}, u32[]{:S(2)}, u32[]{:S(2)}) collective-permute-start(f32[72,1024]{1,0:T(8,128)S(1)} %get-tuple-element.62), channel_id=1, source_target_pairs={{4,0},{5,1},{6,2},{7,3},{8,12},{9,13},{10,14},{11,15},{20,16},{21,... | collective-permute-start | bytes 884744 | tf_op jit(solution)/shard_map/ppermute | solution.py:237
  38.4 19.6 %collective-permute-start.16 = (f32[72,1024]{1,0:T(8,128)S(1)}, f32[72,1024]{1,0:T(8,128)S(1)}, u32[]{:S(2)}, u32[]{:S(2)}) collective-permute-start(f32[72,1024]{1,0:T(8,128)S(1)} %pad_maximum_fusion.6), channel_id=1, source_target_pairs={{1,4},{3,6},{9,12},{11,14},{17,20},{19,22},{25,28},{27,30}} | collective-permute-start | bytes 884744 | tf_op jit(solution)/shard_map/ppermute | solution.py:237
  39.1 18.9 %collective-permute-start.15 = (f32[72,1024]{1,0:T(8,128)S(1)}, f32[72,1024]{1,0:T(8,128)S(1)}, u32[]{:S(2)}, u32[]{:S(2)}) collective-permute-start(f32[72,1024]{1,0:T(8,128)S(1)} %get-tuple-element.61), channel_id=1, source_target_pairs={{1,0},{3,2},{13,8},{15,10},{17,16},{19,18},{29,24},{31,26}} | collective-permute-start | bytes 884744 | tf_op jit(solution)/shard_map/ppermute | solution.py:237
  40.6 9.9 %collective-permute-start.10 = (f32[72,1024]{1,0:T(8,128)S(1)}, f32[72,1024]{1,0:T(8,128)S(1)}, u32[]{:S(2)}, u32[]{:S(2)}) collective-permute-start(f32[72,1024]{1,0:T(8,128)S(1)} %fusion.5.v), channel_id=1, source_target_pairs={{0,8},{4,12},{8,0},{12,4},{16,24},{20,28},{24,16},{28,20},{1,9},{5... | collective-permute-start | bytes 884744 | tf_op jit(solution)/shard_map/ppermute | solution.py:222
  42.1 15.1 %collective-permute-start.9 = (f32[72,1024]{1,0:T(8,128)S(1)}, f32[72,1024]{1,0:T(8,128)S(1)}, u32[]{:S(2)}, u32[]{:S(2)}) collective-permute-start(f32[72,1024]{1,0:T(8,128)S(1)} %fusion.5.v), channel_id=1, source_target_pairs={{0,1},{1,0},{2,3},{3,2},{4,5},{5,4},{6,7},{7,6},{8,9},{9,8},{10,11... | collective-permute-start | bytes 884744 | tf_op jit(solution)/shard_map/ppermute | solution.py:222
  57.3 11.1 %collective-permute-start.12 = (f32[216,1024]{1,0:T(8,128)S(1)}, f32[216,1024]{1,0:T(8,128)S(1)}, u32[]{:S(2)}, u32[]{:S(2)}) collective-permute-start(f32[216,1024]{1,0:T(8,128)S(1)} %pad_maximum_fusion), channel_id=1, source_target_pairs={{0,4},{4,0},{8,12},{12,8},{16,20},{20,16},{24,28},{28,24},{1,5},{5... | collective-permute-start | bytes 2654216 | tf_op jit(solution)/shard_map/ppermute | solution.py:222
  57.4 9.4 %collective-permute-start.11 = (f32[72,1024]{1,0:T(8,128)S(1)}, f32[72,1024]{1,0:T(8,128)S(1)}, u32[]{:S(2)}, u32[]{:S(2)}) collective-permute-start(f32[72,1024]{1,0:T(8,128)S(1)} %collective-permute-done.9.beside), channel_id=1, source_target_pairs={{0,8},{4,12},{8,0},{12,4},{16,24},{20,28},{24,16},{28,20},{1,9},{5... | collective-permute-start | bytes 884744 | tf_op jit(solution)/shard_map/ppermute | solution.py:222
  66.8 1.6 %collective-permute-start.13 = (f32[72,1024]{1,0:T(8,128)S(1)}, f32[72,1024]{1,0:T(8,128)S(1)}, u32[]{:S(2)}, u32[]{:S(2)}) collective-permute-start(f32[72,1024]{1,0:T(8,128)S(1)} %collective-permute-done.11.far_beside), channel_id=1, source_target_pairs={{0,4},{4,0},{8,12},{12,8},{16,20},{20,16},{24,28},{28,24},{1,5},{5... | collective-permute-start | bytes 884744 | tf_op jit(solution)/shard_map/ppermute | solution.py:222
  74.3 3.6 %collective-permute-start.18 = (f32[192]{0:T(256)S(1)}, f32[192]{0:T(256)S(1)}, u32[]{:S(2)}, u32[]{:S(2)}) collective-permute-start(f32[192]{0:T(256)S(1)} %fusion.9), channel_id=1, source_target_pairs={{0,1},{1,0},{2,3},{3,2},{4,5},{5,4},{6,7},{7,6},{8,9},{9,8},{10,11... | collective-permute-start | bytes 2312 | tf_op jit(solution)/shard_map/ppermute | solution.py:222
  79.8 3.9 %collective-permute-start.20 = (f32[768]{0:T(1024)}, f32[768]{0:T(1024)}, u32[]{:S(2)}, u32[]{:S(2)}) collective-permute-start(f32[768]{0:T(1024)} %pad_maximum_fusion.9), channel_id=1, source_target_pairs={{0,8},{4,12},{8,0},{12,4},{16,24},{20,28},{24,16},{28,20},{1,9},{5... | collective-permute-start | bytes 9224 | tf_op jit(solution)/shard_map/ppermute | solution.py:222
  84.5 13.0 %collective-permute-start.21 = (f32[256]{0:T(256)S(1)}, f32[256]{0:T(256)S(1)}, u32[]{:S(2)}, u32[]{:S(2)}) collective-permute-start(f32[256]{0:T(256)S(1)} %get-tuple-element.70), channel_id=1, source_target_pairs={{0,16},{4,20},{8,24},{12,28},{1,17},{5,21},{9,25},{13,29},{2,18},{... | collective-permute-start | bytes 3080 | tf_op jit(solution)/shard_map/ppermute | solution.py:216
  89.0 8.5 %collective-permute-start.22 = (f32[256]{0:T(256)S(1)}, f32[256]{0:T(256)S(1)}, u32[]{:S(2)}, u32[]{:S(2)}) collective-permute-start(f32[256]{0:T(256)S(1)} %get-tuple-element.67), channel_id=1, source_target_pairs={{16,0},{20,4},{24,8},{28,12},{17,1},{21,5},{25,9},{29,13},{18,2},{... | collective-permute-start | bytes 3080 | tf_op jit(solution)/shard_map/ppermute | solution.py:216
  90.3 7.2 %collective-permute-start.23 = (f32[512]{0:T(512)S(1)}, f32[512]{0:T(512)S(1)}, u32[]{:S(2)}, u32[]{:S(2)}) collective-permute-start(f32[512]{0:T(512)S(1)} %pad_maximum_fusion.12), channel_id=1, source_target_pairs={{0,2},{1,3},{4,6},{5,7},{8,10},{9,11},{12,14},{13,15},{16,18},{17,... | collective-permute-start | bytes 6152 | tf_op jit(solution)/shard_map/ppermute | solution.py:216
  93.7 5.5 %collective-permute-start.24 = (f32[512]{0:T(512)S(1)}, f32[512]{0:T(512)S(1)}, u32[]{:S(2)}, u32[]{:S(2)}) collective-permute-start(f32[512]{0:T(512)S(1)} %pad_maximum_fusion.13), channel_id=1, source_target_pairs={{2,0},{3,1},{6,4},{7,5},{10,8},{11,9},{14,12},{15,13},{18,16},{19,... | collective-permute-start | bytes 6152 | tf_op jit(solution)/shard_map/ppermute | solution.py:216
  (14 other events, 81.5 us)

commit v3 on v2

--- a/solution.py
+++ b/solution.py
@@ -276,7 +276,6 @@
     t_ii_o = partner(t_ii, "gx", 0)
     t_ie = partner(after(ie, t_ii), "gy", 0)
     ie_o = partner(ie, "gx", 0)
-    t_ie_o = partner(t_ie, "gx", 0)
     g, gt, h = call(
         gain2,
         flags,
@@ -284,6 +283,7 @@
         [(2 * s, 2 * s), (2 * s, 2 * s), (1, 2 * s)],
         6 * (2 * s) ** 3 * 20,
     )
+    t_ie_o = partner(after(t_ie, g), "gx", 0)
     (merged,) = call(
         apply2,
         flags,

time: 102 us -> 97.5 us (0.956)
  waiting for transfers between devices: 41.5 us -> 37.6 us
    ppermute x16, waiting for transfers between devices: 39.7 us -> 35.8 us  [partner(): return lax.ppermute(value, axis, pairs)]
  transfers between devices with their start and end apart: 25 -> 25, of which waited for: 12 -> 13; matrix products, arithmetic and copies ran while one was open for 4% -> 4% of each run, Pallas kernels for 8% -> 9%
where the time goes in v3:
time: 97.5 us; the launch traced here: 97.1 us
  waiting for transfers between devices  37.6 us (39%)
  starting transfers between devices  29.9 us (31%)
  Pallas kernels  19.1 us (20%)
  other arithmetic  6.15 us (6%)
  local copies, waits for them, and re-layouts  3.22 us (3%)
  between operations  1.19 us (1%)
    ppermute x16, waiting for transfers between devices, partner(): return lax.ppermute(value, axis, pairs)  35.8 us
    pallas_call x5, Pallas kernels, call(): pl.pallas_call(body, out_shape=outs, in_specs=[pl.BlockSpec(memory_space=...  19.1 us
    ppermute x4, starting transfers between devices, from_behind(): return lax.ppermute(block, axis, route)  10.5 us
    ppermute x16, starting transfers between devices, partner(): return lax.ppermute(value, axis, pairs)  10.4 us
    ppermute x5, starting transfers between devices, send(): return lax.ppermute(value, ('gx', 'gy'), pairs)  9 us
  transfers between devices with their start and end apart: 25, of which 13 were waited for; matrix products, arithmetic and copies ran while one was open for 4% of the time, Pallas kernels for 9%

profile of v3, /device:TPU:0, one launch (start us, length us, event | category | flops | bytes accessed | tf_op | source)
XLA Modules:
  0.0 97.1 jit_solution(16317378076583214073)
XLA Ops:
  0.6 1.3 %select_bitcast_fusion.1 = (f32[128,512]{1,0:T(8,128)S(1)}, f32[128,512]{1,0:T(8,128)S(1)}, f32[128,512]{1,0:T(8,128)S(1)}, f32[128,512]{1,0:T(8,128)S(1)}) fusion(f32[1,1,512,512]{3,2,1,0:T(8,128)} %param.4, pred[]{:T(512)} %eq.28), kind=kLoop, calls=%fused_computation.27 | loop fusion | flops 131072 | bytes 2097153 | tf_op jit(solution)/shard_map/jit(_where)/select_n | solution.py:260
  4.3 3.8 %shard_map.59 = (f32[256,512]{1,0:T(8,128)S(1)}, f32[256,256]{1,0:T(8,128)S(1)}, f32[128,512]{1,0:T(8,128)S(1)}, f32[136,256]{1,0:T(8,128)S(1)}, f32[1,256]{1,0:T(1,128)S(1)}) custom-call(s32[3]{0:T(128)S(1)} %add_convert_fusion.flags, f32[512,512]{1,0:T(8,128)S(1)} %fusion.1.own, f32[128,512]{1,0:T(8,128)S(1)} %collective-permute-done.other, ...), custom_call_target="tpu_custom_call" | custom-call | flops 629145600 | bytes 2502144 | tf_op jit(solution)/shard_map/pallas_call | solution.py:202
  8.1 2.9 %collective-permute-start.3 = (f32[136,256]{1,0:T(8,128)S(1)}, f32[136,256]{1,0:T(8,128)S(1)}, u32[]{:S(2)}, u32[]{:S(2)}) collective-permute-start(f32[136,256]{1,0:T(8,128)S(1)} %get-tuple-element.20.mine), channel_id=1, source_target_pairs={{0,1},{1,0},{2,3},{3,2},{4,5},{5,4},{6,7},{7,6},{8,9},{9,8},{10,11... | collective-permute-start | bytes 417800 | tf_op jit(solution)/shard_map/ppermute | solution.py:222
  11.0 4.0 %collective-permute-done.3.t = f32[136,256]{1,0:T(8,128)S(1)} collective-permute-done((f32[136,256]{1,0:T(8,128)S(1)}, f32[136,256]{1,0:T(8,128)S(1)}, u32[]{:S(2)}, u32[]{:S(2)}) %collective-permute-start.3) | collective-permute-done | bytes 139296 | tf_op jit(solution)/shard_map/ppermute | solution.py:222
  15.0 1.7 %collective-permute-start.6 = (f32[128,512]{1,0:T(8,128)S(1)}, f32[128,512]{1,0:T(8,128)S(1)}, u32[]{:S(2)}, u32[]{:S(2)}) collective-permute-start(f32[128,512]{1,0:T(8,128)S(1)} %get-tuple-element.26.mine), channel_id=1, source_target_pairs={{0,1},{1,0},{2,3},{3,2},{4,5},{5,4},{6,7},{7,6},{8,9},{9,8},{10,11... | collective-permute-start | bytes 786440 | tf_op jit(solution)/shard_map/ppermute | solution.py:222
  17.0 5.9 %shard_map.60 = (f32[256,256]{1,0:T(8,128)S(1)}, f32[256,256]{1,0:T(8,128)S(1)}, f32[1,256]{1,0:T(1,128)S(1)}) custom-call(s32[3]{0:T(128)S(1)} %add_convert_fusion.flags, f32[136,256]{1,0:T(8,128)S(1)} %get-tuple-element.20.mine, f32[136,256]{1,0:T(8,128)S(1)} %collective-permute-done.2.mine_o, f32[136,256]{1,0:T(8,128)S(1)} %collective-permute-done.3.t, ...), custom_call_target="tpu_custom_call" | custom-call | flops 2013265920 | bytes 1345536 | tf_op jit(solution)/shard_map/pallas_call | solution.py:202
  27.4 5.1 %collective-permute-start.14 = (f32[136,1024]{1,0:T(8,128)S(1)}, f32[136,1024]{1,0:T(8,128)S(1)}, u32[]{:S(2)}, u32[]{:S(2)}) collective-permute-start(f32[136,1024]{1,0:T(8,128)S(1)} %maximum_select_fusion.2), channel_id=1, source_target_pairs={{0,1},{2,3},{8,9},{10,11},{12,8},{14,10},{16,17},{18,19},{24,25},{... | collective-permute-start | bytes 1671176 | tf_op jit(solution)/shard_map/ppermute | solution.py:237
  32.8 1.3 %collective-permute-start.8 = (f32[72,1024]{1,0:T(8,128)S(1)}, f32[72,1024]{1,0:T(8,128)S(1)}, u32[]{:S(2)}, u32[]{:S(2)}) collective-permute-start(f32[72,1024]{1,0:T(8,128)S(1)} %get-tuple-element.64), channel_id=1, source_target_pairs={{4,0},{5,1},{6,2},{7,3},{8,12},{9,13},{10,14},{11,15},{20,16},{21,... | collective-permute-start | bytes 884744 | tf_op jit(solution)/shard_map/ppermute | solution.py:237
  34.8 1.3 %collective-permute-start.15 = (f32[72,1024]{1,0:T(8,128)S(1)}, f32[72,1024]{1,0:T(8,128)S(1)}, u32[]{:S(2)}, u32[]{:S(2)}) collective-permute-start(f32[72,1024]{1,0:T(8,128)S(1)} %get-tuple-element.63), channel_id=1, source_target_pairs={{1,0},{3,2},{13,8},{15,10},{17,16},{19,18},{29,24},{31,26}} | collective-permute-start | bytes 884744 | tf_op jit(solution)/shard_map/ppermute | solution.py:237
  36.3 1.5 %collective-permute-start.10 = (f32[72,1024]{1,0:T(8,128)S(1)}, f32[72,1024]{1,0:T(8,128)S(1)}, u32[]{:S(2)}, u32[]{:S(2)}) collective-permute-start(f32[72,1024]{1,0:T(8,128)S(1)} %fusion.5.v), channel_id=1, source_target_pairs={{0,8},{4,12},{8,0},{12,4},{16,24},{20,28},{24,16},{28,20},{1,9},{5... | collective-permute-start | bytes 884744 | tf_op jit(solution)/shard_map/ppermute | solution.py:222
  37.8 2.6 %collective-permute-start.9 = (f32[72,1024]{1,0:T(8,128)S(1)}, f32[72,1024]{1,0:T(8,128)S(1)}, u32[]{:S(2)}, u32[]{:S(2)}) collective-permute-start(f32[72,1024]{1,0:T(8,128)S(1)} %fusion.5.v), channel_id=1, source_target_pairs={{0,1},{1,0},{2,3},{3,2},{4,5},{5,4},{6,7},{7,6},{8,9},{9,8},{10,11... | collective-permute-start | bytes 884744 | tf_op jit(solution)/shard_map/ppermute | solution.py:222
  41.1 5.0 %collective-permute-done.10.far = f32[72,1024]{1,0:T(8,128)S(1)} collective-permute-done((f32[72,1024]{1,0:T(8,128)S(1)}, f32[72,1024]{1,0:T(8,128)S(1)}, u32[]{:S(2)}, u32[]{:S(2)}) %collective-permute-start.10) | collective-permute-done | bytes 294944 | tf_op jit(solution)/shard_map/ppermute | solution.py:222
  46.1 6.8 %collective-permute-done.9.beside = f32[72,1024]{1,0:T(8,128)S(1)} collective-permute-done((f32[72,1024]{1,0:T(8,128)S(1)}, f32[72,1024]{1,0:T(8,128)S(1)}, u32[]{:S(2)}, u32[]{:S(2)}) %collective-permute-start.9) | collective-permute-done | bytes 294944 | tf_op jit(solution)/shard_map/ppermute | solution.py:222
  54.2 8.3 %collective-permute-done.11.far_beside = f32[72,1024]{1,0:T(8,128)S(1)} collective-permute-done((f32[72,1024]{1,0:T(8,128)S(1)}, f32[72,1024]{1,0:T(8,128)S(1)}, u32[]{:S(2)}, u32[]{:S(2)}) %collective-permute-start.11) | collective-permute-done | bytes 294944 | tf_op jit(solution)/shard_map/ppermute | solution.py:222
  64.1 5.9 %shard_map.62 = (f32[192,256]{1,0:T(8,128)S(1)}, f32[192,256]{1,0:T(8,128)S(1)}, f32[1,256]{1,0:T(1,128)S(1)}) custom-call(s32[3]{0:T(128)S(1)} %add_convert_fusion.flags, f32[72,1024]{1,0:T(8,128)S(1)} %fusion.5.v, f32[72,1024]{1,0:T(8,128)S(1)} %collective-permute-done.9.beside, f32[72,1024]{1,0:T(8,128)S(1)} %collective-permute-done.10.far, ...), custom_call_target="tpu_custom_call" | custom-call | flops 2013265920 | bytes 3539968 | tf_op jit(solution)/shard_map/pallas_call | solution.py:202
  70.1 3.6 %collective-permute-done.18 = f32[192]{0:T(256)S(1)} collective-permute-done((f32[192]{0:T(256)S(1)}, f32[192]{0:T(256)S(1)}, u32[]{:S(2)}, u32[]{:S(2)}) %collective-permute-start.18) | collective-permute-done | bytes 800 | tf_op jit(solution)/shard_map/ppermute | solution.py:222
  75.8 3.7 %collective-permute-done.20 = f32[768]{0:T(1024)} collective-permute-done((f32[768]{0:T(1024)}, f32[768]{0:T(1024)}, u32[]{:S(2)}, u32[]{:S(2)}) %collective-permute-start.20) | collective-permute-done | bytes 3104 | tf_op jit(solution)/shard_map/ppermute | solution.py:222
  80.2 4.5 %collective-permute-start.21 = (f32[256]{0:T(256)S(1)}, f32[256]{0:T(256)S(1)}, u32[]{:S(2)}, u32[]{:S(2)}) collective-permute-start(f32[256]{0:T(256)S(1)} %get-tuple-element.72), channel_id=1, source_target_pairs={{0,16},{4,20},{8,24},{12,28},{1,17},{5,21},{9,25},{13,29},{2,18},{... | collective-permute-start | bytes 3080 | tf_op jit(solution)/shard_map/ppermute | solution.py:216
  84.7 1.3 %collective-permute-start.22 = (f32[256]{0:T(256)S(1)}, f32[256]{0:T(256)S(1)}, u32[]{:S(2)}, u32[]{:S(2)}) collective-permute-start(f32[256]{0:T(256)S(1)} %get-tuple-element.69), channel_id=1, source_target_pairs={{16,0},{20,4},{24,8},{28,12},{17,1},{21,5},{25,9},{29,13},{18,2},{... | collective-permute-start | bytes 3080 | tf_op jit(solution)/shard_map/ppermute | solution.py:216
  86.0 3.4 %collective-permute-start.23 = (f32[512]{0:T(512)S(1)}, f32[512]{0:T(512)S(1)}, u32[]{:S(2)}, u32[]{:S(2)}) collective-permute-start(f32[512]{0:T(512)S(1)} %pad_maximum_fusion.12), channel_id=1, source_target_pairs={{0,2},{1,3},{4,6},{5,7},{8,10},{9,11},{12,14},{13,15},{16,18},{17,... | collective-permute-start | bytes 6152 | tf_op jit(solution)/shard_map/ppermute | solution.py:216
  89.4 1.3 %collective-permute-start.24 = (f32[512]{0:T(512)S(1)}, f32[512]{0:T(512)S(1)}, u32[]{:S(2)}, u32[]{:S(2)}) collective-permute-start(f32[512]{0:T(512)S(1)} %pad_maximum_fusion.13), channel_id=1, source_target_pairs={{2,0},{3,1},{6,4},{7,5},{10,8},{11,9},{14,12},{15,13},{18,16},{19,... | collective-permute-start | bytes 6152 | tf_op jit(solution)/shard_map/ppermute | solution.py:216
  90.8 2.4 %shard_map.63 = f32[192,1536]{1,0:T(8,128)} custom-call(s32[3]{0:T(128)S(1)} %add_convert_fusion.flags, f32[72,1024]{1,0:T(8,128)S(1)} %fusion.5.v, f32[72,1024]{1,0:T(8,128)S(1)} %collective-permute-done.9.beside, f32[72,1024]{1,0:T(8,128)S(1)} %collective-permute-done.10.far, f32[72,1024]{1,0:T(8,128)S(1)} %collective-permute-done.11.far_beside, ...), custom_call_target="tpu_custom_call" | custom-call | flops 452984832 | bytes 4718592 | tf_op jit(solution)/shard_map/pallas_call | solution.py:202
  93.2 1.7 %collective-permute-done.24 = f32[512]{0:T(512)S(1)} collective-permute-done((f32[512]{0:T(512)S(1)}, f32[512]{0:T(512)S(1)}, u32[]{:S(2)}, u32[]{:S(2)}) %collective-permute-start.24) | collective-permute-done | bytes 2080 | tf_op jit(solution)/shard_map/ppermute | solution.py:216
  95.0 1.4 %multiply_reduce_fusion = f32[192]{0:T(256)S(1)} fusion(f32[192,1536]{1,0:T(8,128)} %shard_map.63, f32[1536]{0:T(1024)S(1)} %negate_multiply_fusion), kind=kLoop, calls=%fused_computation.2 | loop fusion | flops 589632 | bytes 1186560 | tf_op jit(solution)/shard_map/reduce_sum | solution.py:408
  (115 shorter events, 15.4 us)
Async XLA Ops:
  2.2 2.2 %collective-permute-start = (f32[128,512]{1,0:T(8,128)S(1)}, f32[128,512]{1,0:T(8,128)S(1)}, u32[]{:S(2)}, u32[]{:S(2)}) collective-permute-start(f32[128,512]{1,0:T(8,128)S(1)} %slice.140), channel_id=1, source_target_pairs={{0,4},{4,0},{8,12},{12,8},{16,20},{20,16},{24,28},{28,24},{1,5},{5... | collective-permute-start | bytes 786440 | tf_op jit(solution)/shard_map/ppermute | solution.py:222
  3.0 1.3 %collective-permute-start.1 = (f32[1,128]{1,0:T(1,128)S(1)}, f32[1,128]{1,0:T(1,128)S(1)}, u32[]{:S(2)}, u32[]{:S(2)}) collective-permute-start(f32[1,128]{1,0:T(1,128)S(1)} %slice.141), channel_id=1, source_target_pairs={{0,4},{4,0},{8,12},{12,8},{16,20},{20,16},{24,28},{28,24},{1,5},{5... | collective-permute-start | bytes 1544 | tf_op jit(solution)/shard_map/ppermute | solution.py:222
  8.1 6.9 %collective-permute-start.3 = (f32[136,256]{1,0:T(8,128)S(1)}, f32[136,256]{1,0:T(8,128)S(1)}, u32[]{:S(2)}, u32[]{:S(2)}) collective-permute-start(f32[136,256]{1,0:T(8,128)S(1)} %get-tuple-element.20.mine), channel_id=1, source_target_pairs={{0,1},{1,0},{2,3},{3,2},{4,5},{5,4},{6,7},{7,6},{8,9},{9,8},{10,11... | collective-permute-start | bytes 417800 | tf_op jit(solution)/shard_map/ppermute | solution.py:222
  11.0 6.0 %collective-permute-start.2 = (f32[136,256]{1,0:T(8,128)S(1)}, f32[136,256]{1,0:T(8,128)S(1)}, u32[]{:S(2)}, u32[]{:S(2)}) collective-permute-start(f32[136,256]{1,0:T(8,128)S(1)} %get-tuple-element.20.mine), channel_id=1, source_target_pairs={{0,4},{4,0},{8,12},{12,8},{16,20},{20,16},{24,28},{28,24},{1,5},{5... | collective-permute-start | bytes 417800 | tf_op jit(solution)/shard_map/ppermute | solution.py:222
  15.0 2.0 %collective-permute-start.4 = (f32[136,256]{1,0:T(8,128)S(1)}, f32[136,256]{1,0:T(8,128)S(1)}, u32[]{:S(2)}, u32[]{:S(2)}) collective-permute-start(f32[136,256]{1,0:T(8,128)S(1)} %collective-permute-done.3.t), channel_id=1, source_target_pairs={{0,4},{4,0},{8,12},{12,8},{16,20},{20,16},{24,28},{28,24},{1,5},{5... | collective-permute-start | bytes 417800 | tf_op jit(solution)/shard_map/ppermute | solution.py:222
  15.0 8.7 %collective-permute-start.6 = (f32[128,512]{1,0:T(8,128)S(1)}, f32[128,512]{1,0:T(8,128)S(1)}, u32[]{:S(2)}, u32[]{:S(2)}) collective-permute-start(f32[128,512]{1,0:T(8,128)S(1)} %get-tuple-element.26.mine), channel_id=1, source_target_pairs={{0,1},{1,0},{2,3},{3,2},{4,5},{5,4},{6,7},{7,6},{8,9},{9,8},{10,11... | collective-permute-start | bytes 786440 | tf_op jit(solution)/shard_map/ppermute | solution.py:222
  16.8 7.6 %collective-permute-start.5 = (f32[128,512]{1,0:T(8,128)S(1)}, f32[128,512]{1,0:T(8,128)S(1)}, u32[]{:S(2)}, u32[]{:S(2)}) collective-permute-start(f32[128,512]{1,0:T(8,128)S(1)} %get-tuple-element.26.mine), channel_id=1, source_target_pairs={{0,4},{4,0},{8,12},{12,8},{16,20},{20,16},{24,28},{28,24},{1,5},{5... | collective-permute-start | bytes 786440 | tf_op jit(solution)/shard_map/ppermute | solution.py:222
  23.7 1.5 %collective-permute-start.7 = (f32[128,512]{1,0:T(8,128)S(1)}, f32[128,512]{1,0:T(8,128)S(1)}, u32[]{:S(2)}, u32[]{:S(2)}) collective-permute-start(f32[128,512]{1,0:T(8,128)S(1)} %collective-permute-done.6.t), channel_id=1, source_target_pairs={{0,4},{4,0},{8,12},{12,8},{16,20},{20,16},{24,28},{28,24},{1,5},{5... | collective-permute-start | bytes 786440 | tf_op jit(solution)/shard_map/ppermute | solution.py:222
  26.6 5.9 %collective-permute-start.17 = (f32[72,1024]{1,0:T(8,128)S(1)}, f32[72,1024]{1,0:T(8,128)S(1)}, u32[]{:S(2)}, u32[]{:S(2)}) collective-permute-start(f32[72,1024]{1,0:T(8,128)S(1)} %fusion.4), channel_id=1, source_target_pairs={{1,5},{3,7},{9,13},{11,15},{13,9},{15,11},{17,21},{19,23},{25,29},... | collective-permute-start | bytes 884744 | tf_op jit(solution)/shard_map/ppermute | solution.py:237
  27.4 13.5 %collective-permute-start.14 = (f32[136,1024]{1,0:T(8,128)S(1)}, f32[136,1024]{1,0:T(8,128)S(1)}, u32[]{:S(2)}, u32[]{:S(2)}) collective-permute-start(f32[136,1024]{1,0:T(8,128)S(1)} %maximum_select_fusion.2), channel_id=1, source_target_pairs={{0,1},{2,3},{8,9},{10,11},{12,8},{14,10},{16,17},{18,19},{24,25},{... | collective-permute-start | bytes 1671176 | tf_op jit(solution)/shard_map/ppermute | solution.py:237
  32.8 3.5 %collective-permute-start.8 = (f32[72,1024]{1,0:T(8,128)S(1)}, f32[72,1024]{1,0:T(8,128)S(1)}, u32[]{:S(2)}, u32[]{:S(2)}) collective-permute-start(f32[72,1024]{1,0:T(8,128)S(1)} %get-tuple-element.64), channel_id=1, source_target_pairs={{4,0},{5,1},{6,2},{7,3},{8,12},{9,13},{10,14},{11,15},{20,16},{21,... | collective-permute-start | bytes 884744 | tf_op jit(solution)/shard_map/ppermute | solution.py:237
  34.1 19.6 %collective-permute-start.16 = (f32[72,1024]{1,0:T(8,128)S(1)}, f32[72,1024]{1,0:T(8,128)S(1)}, u32[]{:S(2)}, u32[]{:S(2)}) collective-permute-start(f32[72,1024]{1,0:T(8,128)S(1)} %pad_maximum_fusion.6), channel_id=1, source_target_pairs={{1,4},{3,6},{9,12},{11,14},{17,20},{19,22},{25,28},{27,30}} | collective-permute-start | bytes 884744 | tf_op jit(solution)/shard_map/ppermute | solution.py:237
  34.8 18.9 %collective-permute-start.15 = (f32[72,1024]{1,0:T(8,128)S(1)}, f32[72,1024]{1,0:T(8,128)S(1)}, u32[]{:S(2)}, u32[]{:S(2)}) collective-permute-start(f32[72,1024]{1,0:T(8,128)S(1)} %get-tuple-element.63), channel_id=1, source_target_pairs={{1,0},{3,2},{13,8},{15,10},{17,16},{19,18},{29,24},{31,26}} | collective-permute-start | bytes 884744 | tf_op jit(solution)/shard_map/ppermute | solution.py:237
  36.3 9.9 %collective-permute-start.10 = (f32[72,1024]{1,0:T(8,128)S(1)}, f32[72,1024]{1,0:T(8,128)S(1)}, u32[]{:S(2)}, u32[]{:S(2)}) collective-permute-start(f32[72,1024]{1,0:T(8,128)S(1)} %fusion.5.v), channel_id=1, source_target_pairs={{0,8},{4,12},{8,0},{12,4},{16,24},{20,28},{24,16},{28,20},{1,9},{5... | collective-permute-start | bytes 884744 | tf_op jit(solution)/shard_map/ppermute | solution.py:222
  37.8 15.1 %collective-permute-start.9 = (f32[72,1024]{1,0:T(8,128)S(1)}, f32[72,1024]{1,0:T(8,128)S(1)}, u32[]{:S(2)}, u32[]{:S(2)}) collective-permute-start(f32[72,1024]{1,0:T(8,128)S(1)} %fusion.5.v), channel_id=1, source_target_pairs={{0,1},{1,0},{2,3},{3,2},{4,5},{5,4},{6,7},{7,6},{8,9},{9,8},{10,11... | collective-permute-start | bytes 884744 | tf_op jit(solution)/shard_map/ppermute | solution.py:222
  53.0 11.1 %collective-permute-start.12 = (f32[216,1024]{1,0:T(8,128)S(1)}, f32[216,1024]{1,0:T(8,128)S(1)}, u32[]{:S(2)}, u32[]{:S(2)}) collective-permute-start(f32[216,1024]{1,0:T(8,128)S(1)} %pad_maximum_fusion), channel_id=1, source_target_pairs={{0,4},{4,0},{8,12},{12,8},{16,20},{20,16},{24,28},{28,24},{1,5},{5... | collective-permute-start | bytes 2654216 | tf_op jit(solution)/shard_map/ppermute | solution.py:222
  53.1 9.4 %collective-permute-start.11 = (f32[72,1024]{1,0:T(8,128)S(1)}, f32[72,1024]{1,0:T(8,128)S(1)}, u32[]{:S(2)}, u32[]{:S(2)}) collective-permute-start(f32[72,1024]{1,0:T(8,128)S(1)} %collective-permute-done.9.beside), channel_id=1, source_target_pairs={{0,8},{4,12},{8,0},{12,4},{16,24},{20,28},{24,16},{28,20},{1,9},{5... | collective-permute-start | bytes 884744 | tf_op jit(solution)/shard_map/ppermute | solution.py:222
  62.5 1.6 %collective-permute-start.13 = (f32[72,1024]{1,0:T(8,128)S(1)}, f32[72,1024]{1,0:T(8,128)S(1)}, u32[]{:S(2)}, u32[]{:S(2)}) collective-permute-start(f32[72,1024]{1,0:T(8,128)S(1)} %collective-permute-done.11.far_beside), channel_id=1, source_target_pairs={{0,4},{4,0},{8,12},{12,8},{16,20},{20,16},{24,28},{28,24},{1,5},{5... | collective-permute-start | bytes 884744 | tf_op jit(solution)/shard_map/ppermute | solution.py:222
  70.1 3.6 %collective-permute-start.18 = (f32[192]{0:T(256)S(1)}, f32[192]{0:T(256)S(1)}, u32[]{:S(2)}, u32[]{:S(2)}) collective-permute-start(f32[192]{0:T(256)S(1)} %fusion.9), channel_id=1, source_target_pairs={{0,1},{1,0},{2,3},{3,2},{4,5},{5,4},{6,7},{7,6},{8,9},{9,8},{10,11... | collective-permute-start | bytes 2312 | tf_op jit(solution)/shard_map/ppermute | solution.py:222
  75.6 3.9 %collective-permute-start.20 = (f32[768]{0:T(1024)}, f32[768]{0:T(1024)}, u32[]{:S(2)}, u32[]{:S(2)}) collective-permute-start(f32[768]{0:T(1024)} %pad_maximum_fusion.9), channel_id=1, source_target_pairs={{0,8},{4,12},{8,0},{12,4},{16,24},{20,28},{24,16},{28,20},{1,9},{5... | collective-permute-start | bytes 9224 | tf_op jit(solution)/shard_map/ppermute | solution.py:222
  80.2 13.0 %collective-permute-start.21 = (f32[256]{0:T(256)S(1)}, f32[256]{0:T(256)S(1)}, u32[]{:S(2)}, u32[]{:S(2)}) collective-permute-start(f32[256]{0:T(256)S(1)} %get-tuple-element.72), channel_id=1, source_target_pairs={{0,16},{4,20},{8,24},{12,28},{1,17},{5,21},{9,25},{13,29},{2,18},{... | collective-permute-start | bytes 3080 | tf_op jit(solution)/shard_map/ppermute | solution.py:216
  84.7 8.5 %collective-permute-start.22 = (f32[256]{0:T(256)S(1)}, f32[256]{0:T(256)S(1)}, u32[]{:S(2)}, u32[]{:S(2)}) collective-permute-start(f32[256]{0:T(256)S(1)} %get-tuple-element.69), channel_id=1, source_target_pairs={{16,0},{20,4},{24,8},{28,12},{17,1},{21,5},{25,9},{29,13},{18,2},{... | collective-permute-start | bytes 3080 | tf_op jit(solution)/shard_map/ppermute | solution.py:216
  86.0 7.2 %collective-permute-start.23 = (f32[512]{0:T(512)S(1)}, f32[512]{0:T(512)S(1)}, u32[]{:S(2)}, u32[]{:S(2)}) collective-permute-start(f32[512]{0:T(512)S(1)} %pad_maximum_fusion.12), channel_id=1, source_target_pairs={{0,2},{1,3},{4,6},{5,7},{8,10},{9,11},{12,14},{13,15},{16,18},{17,... | collective-permute-start | bytes 6152 | tf_op jit(solution)/shard_map/ppermute | solution.py:216
  89.4 5.5 %collective-permute-start.24 = (f32[512]{0:T(512)S(1)}, f32[512]{0:T(512)S(1)}, u32[]{:S(2)}, u32[]{:S(2)}) collective-permute-start(f32[512]{0:T(512)S(1)} %pad_maximum_fusion.13), channel_id=1, source_target_pairs={{2,0},{3,1},{6,4},{7,5},{10,8},{11,9},{14,12},{15,13},{18,16},{19,... | collective-permute-start | bytes 6152 | tf_op jit(solution)/shard_map/ppermute | solution.py:216
  (14 other events, 81.5 us)
